TPU v7x, 256 devices: a whole 4x4x8 slice. The times are simulated.
256 devices in a mesh: tm: 128 (over z, y, x), space: 2 (over core).
Axes of the slice: x: 4, y: 4, z: 8, core: 2. Of those that a mesh axis runs over, the one named last changes fastest.
Arguments:
- features: bfloat16 [256, 128, 2048], P('tm', 'space'), may hold values from -24 to 24
- queries: bfloat16 [256, 128, 1024], P('tm', 'space'), may hold values from -144 to 144
- cotangent: bfloat16 [256, 128, 1024], P('tm', 'space'), may hold values from -6 to 6
- key_weight: bfloat16 [2048, 1024], P(None, 'space'), may hold values from -0.125 to 0.125
- value_weight: bfloat16 [2048, 1024], P(None, 'space'), may hold values from -0.125 to 0.125
Outputs:
- attended: bfloat16 [256, 128, 1024], P('tm', 'space')
- grad_features: bfloat16 [256, 128, 2048], P('tm', 'space')
- grad_queries: bfloat16 [256, 128, 1024], P('tm', 'space')
- grad_key_weight: float32 [2048, 1024], P('tm', 'space')
- grad_value_weight: float32 [2048, 1024], P('tm', 'space')
All inputs are finite; a program needn't handle non-finite values.
Results may differ from a plain program's by a relative error of at most 0.025.
The roundings to bfloat16 on the way count: a program that leaves them out, or rounds other values in their place, can miss the bound.
Values may be sent and summed in bfloat16 or wider, within the bound.
A program may use at most 128 MiB of HBM per device.

v0:
```python
import jax
import jax.numpy as jnp
from jax import lax
from jax.sharding import PartitionSpec as P

HEAD = 128
WINDOW = 16


def passed_along(value, axis, steps):
    count = lax.axis_size(axis)
    initial, last = (max(0, -steps), min(count, count - steps))
    return lax.ppermute(value, axis, [(source, source + steps) for source in range(initial, last)])


def window_allowed(query_pos, key_pos, reach_back, lowest):
    later = key_pos[None, :] <= query_pos[:, None]
    inside = key_pos[None, :] >= query_pos[:, None] - reach_back
    return later & inside & (key_pos[None, :] >= lowest)


def attend(queries_in, grad_out, key_rows, value_rows, allowed):
    scale = queries_in.shape[-1] ** (-0.5)
    scores = (
        jnp.einsum("tphe,uphe->phtu", queries_in, key_rows, preferred_element_type=jnp.float32)
        * scale
    )
    scores = jnp.where(allowed, scores, -jnp.inf)
    row_top = jnp.max(scores, axis=-1, keepdims=True)
    row_total = jnp.log(jnp.sum(jnp.exp(scores - row_top), axis=-1, keepdims=True)) + row_top
    weights = jnp.exp(scores - row_total)
    rounded = weights.astype(jnp.bfloat16)
    dprobs = jnp.einsum("tphe,uphe->phtu", grad_out, value_rows, preferred_element_type=jnp.float32)
    spread = jnp.sum(weights * dprobs, axis=-1, keepdims=True)
    dscore = (weights * (dprobs - spread) * scale).astype(jnp.bfloat16)
    grad_keys = jnp.einsum(
        "phtu,tphe->uphe", dscore, queries_in, preferred_element_type=jnp.float32
    )
    grad_values = jnp.einsum(
        "phtu,tphe->uphe", rounded, grad_out, preferred_element_type=jnp.float32
    )
    return (rounded, dscore, grad_keys, grad_values, row_total, spread)


def shards(features, queries, cotangent, key_weight, value_weight):
    frames = features.shape[0]
    width_model = features.shape[2]
    half_width = key_weight.shape[1]
    head_local = half_width // HEAD
    reach_back = WINDOW - 1
    hop_count = (reach_back + frames - 1) // frames
    widths = [
        min(frames, reach_back - (hop_index - 1) * frames) for hop_index in range(1, hop_count + 1)
    ]
    all_rows = lax.all_gather(features, "space", axis=1, tiled=True)
    patches = all_rows.shape[1]
    query_heads, cot_heads = (
        lax.all_to_all(queries, "space", split_axis=2, concat_axis=1, tiled=True),
        lax.all_to_all(cotangent, "space", split_axis=2, concat_axis=1, tiled=True),
    )
    key_rows = jnp.dot(all_rows, key_weight, preferred_element_type=jnp.float32).astype(
        jnp.bfloat16
    )
    value_rows = jnp.dot(all_rows, value_weight, preferred_element_type=jnp.float32).astype(
        jnp.bfloat16
    )
    joined = jnp.concatenate([key_rows, value_rows], axis=2)
    pieces = []
    moving = joined
    for hop_index in range(1, hop_count + 1):
        width_now = widths[hop_index - 1]
        moving = passed_along(moving[moving.shape[0] - width_now :], "tm", 1)
        pieces.append(moving)
    extended = jnp.concatenate(list(reversed(pieces)) + [joined], axis=0)
    span_rows = extended.shape[0]
    ext_keys = extended[:, :, :half_width].reshape(span_rows, patches, head_local, HEAD)
    ext_values = extended[:, :, half_width:].reshape(span_rows, patches, head_local, HEAD)
    query_four = query_heads.reshape(frames, patches, head_local, HEAD)
    cot_four = cot_heads.reshape(frames, patches, head_local, HEAD)
    position = lax.axis_index("tm")
    query_pos = jnp.arange(frames, dtype=jnp.int32) + reach_back
    key_pos = jnp.arange(span_rows, dtype=jnp.int32)
    allowed = window_allowed(query_pos, key_pos, reach_back, reach_back - position * frames)
    rounded, dscore, grad_ext_keys, grad_ext_values, row_total, spread = attend(
        query_four, cot_four, ext_keys, ext_values, allowed
    )
    attended_heads = jnp.einsum(
        "phtu,uphe->tphe", rounded, ext_values, preferred_element_type=jnp.float32
    )
    attended_heads = attended_heads.astype(jnp.bfloat16).reshape(frames, patches, half_width)
    attended = lax.all_to_all(attended_heads, "space", split_axis=1, concat_axis=2, tiled=True)
    grad_query_heads = jnp.einsum(
        "phtu,uphe->tphe", dscore, ext_keys, preferred_element_type=jnp.float32
    )
    grad_query_heads = grad_query_heads.astype(jnp.bfloat16).reshape(frames, patches, half_width)
    grad_pairs = jnp.concatenate(
        [
            grad_ext_keys.reshape(span_rows, patches, half_width),
            grad_ext_values.reshape(span_rows, patches, half_width),
        ],
        axis=2,
    )
    own_grads = grad_pairs[reach_back:]
    offset = reach_back
    for hop_index in range(1, hop_count + 1):
        width_now = widths[hop_index - 1]
        offset = offset - width_now
        returned = passed_along(grad_pairs[offset : offset + width_now], "tm", -hop_index)
        own_grads = own_grads.at[frames - width_now :].add(returned)
    grad_queries = lax.all_to_all(
        grad_query_heads, "space", split_axis=1, concat_axis=2, tiled=True
    )
    grad_keys = own_grads[:, :, :half_width].astype(jnp.bfloat16)
    grad_values = own_grads[:, :, half_width:].astype(jnp.bfloat16)
    contract_last = (((2,), (1,)), ((), ()))
    partial_features = lax.dot_general(
        grad_keys, key_weight, contract_last, preferred_element_type=jnp.float32
    )
    partial_features = partial_features + lax.dot_general(
        grad_values, value_weight, contract_last, preferred_element_type=jnp.float32
    )
    grad_features = lax.psum_scatter(
        partial_features, "space", scatter_dimension=1, tiled=True
    ).astype(jnp.bfloat16)
    flat_rows = all_rows.reshape(frames * patches, width_model)
    flat_keys = grad_keys.reshape(frames * patches, half_width)
    flat_values = grad_values.reshape(frames * patches, half_width)
    contract_first = (((0,), (0,)), ((), ()))
    key_part = lax.dot_general(
        flat_rows, flat_keys, contract_first, preferred_element_type=jnp.float32
    )
    value_part = lax.dot_general(
        flat_rows, flat_values, contract_first, preferred_element_type=jnp.float32
    )
    weight_grads = lax.psum_scatter(
        jnp.concatenate([key_part, value_part], axis=1), "tm", scatter_dimension=0, tiled=True
    )
    return (
        attended,
        grad_features,
        grad_queries,
        weight_grads[:, :half_width],
        weight_grads[:, half_width:],
    )


def solution(mesh):
    return jax.shard_map(
        shards,
        mesh=mesh,
        in_specs=(
            P("tm", "space", None),
            P("tm", "space", None),
            P("tm", "space", None),
            P(None, "space"),
            P(None, "space"),
        ),
        out_specs=(
            P("tm", "space", None),
            P("tm", "space", None),
            P("tm", "space", None),
            P("tm", "space"),
            P("tm", "space"),
        ),
        check_vma=False,
    )
```

profile of v0, /device:TPU:0, one launch (start us, length us, event | category | flops | bytes accessed | tf_op | source)
XLA Modules:
  0.0 1412.9 jit_solution(15878651814792615165)
XLA Ops:
  7.9 17.8 %all-gather.2.cloned.1.call-done = bf16[2,128,2048]{2,1,0:T(8,128)(2,1)} async-done(((bf16[2,64,2048]{2,1,0:T(8,128)(2,1)}), bf16[2,128,2048]{2,1,0:T(8,128)(2,1)}) %all-gather.2.cloned.1.call-update) | async-done | bytes 1048592 | tf_op jit(solution)/shard_map/all_gather | solution.py:55
  33.6 11.6 collective-permute-done
  49.6 10.8 collective-permute-done.1
  64.8 9.9 collective-permute-done.2
  79.1 8.9 collective-permute-done.3
  92.5 8.0 collective-permute-done.4
  100.5 6.1 collective-permute-start.5
  106.6 6.3 collective-permute-done.5
  113.0 6.5 collective-permute-start.6
  127.2 7.2 collective-permute-start.7
  170.4 5.3 convolution_bitcast_fusion.2
  175.7 26.6 %convolution_bitcast_fusion.3 = f32[17,128,4,128]{3,0,2,1:T(8,128)} fusion(f32[128,4,2,17]{3,2,1,0:T(2,128)} %fusion.16, bf16[2,128,4,128]{3,2,1,0:T(4,128)(2,1)S(1)} %copy-done.18, f32[128,4,2,17]{3,2,1,0:T(2,128)S(1)} %get-tuple-element.189, f32[128,4,2]{2,1,0:T(4,128)S(1)} %bitcast.87), kind=kOutput, calls=%fused_computation.30 | convolution fusion | flops 4579344 | bytes 4861952 | tf_op jit(solution)/shard_map/phtu,tphe->uphe/dot_general | solution.py:36
  202.3 5.9 copy.78
  208.3 5.7 copy.81
  214.0 5.9 copy.80
  219.9 5.8 copy.82
  236.0 23.1 %collective-permute-done.8 = f32[2,128,1024]{2,1,0:T(8,128)S(1)} collective-permute-done((f32[2,128,1024]{2,1,0:T(8,128)S(1)}, f32[2,128,1024]{2,1,0:T(8,128)S(1)}, u32[]{:S(2)}, u32[]{:S(2)}) %collective-permute-start.8) | collective-permute-done | bytes 1048608 | tf_op jit(solution)/shard_map/ppermute | solution.py:13
  260.3 5.5 collective-permute-done.9
  267.2 21.0 %collective-permute-done.10 = f32[2,128,1024]{2,1,0:T(8,128)S(1)} collective-permute-done((f32[2,128,1024]{2,1,0:T(8,128)S(1)}, f32[2,128,1024]{2,1,0:T(8,128)S(1)}, u32[]{:S(2)}, u32[]{:S(2)}) %collective-permute-start.10) | collective-permute-done | bytes 1048608 | tf_op jit(solution)/shard_map/ppermute | solution.py:13
  289.5 100.3 %collective-permute-done.12 = f32[2,128,1024]{2,1,0:T(8,128)S(1)} collective-permute-done((f32[2,128,1024]{2,1,0:T(8,128)S(1)}, f32[2,128,1024]{2,1,0:T(8,128)S(1)}, u32[]{:S(2)}, u32[]{:S(2)}) %collective-permute-start.12) | collective-permute-done | bytes 1048608 | tf_op jit(solution)/shard_map/ppermute | solution.py:13
  401.1 9.3 copy.94
  410.5 24.4 %fusion.44 = bf16[2,128,4,128]{3,0,2,1:T(2,128)(2,1)S(1)} fusion(bf16[17,128,4,128]{3,2,1,0:T(4,128)(2,1)} %reshape.319, f32[128,4,2,17]{3,2,1,0:T(2,128)} %fusion.16, f32[128,4,2,17]{3,2,1,0:T(2,128)S(1)} %get-tuple-element.189, f32[128,4,2]{2,1,0:T(4,128)S(1)} %bitcast.88), kind=kOutput, calls=%fused_computation.50 | convolution fusion | flops 4710416 | bytes 2633728 | tf_op jit(solution)/shard_map/phtu,uphe->tphe/dot_general | solution.py:92
  450.2 239.4 %reduce-scatter.5.cloned.1.call-done = f32[2,64,2048]{2,1,0:T(8,128)} async-done(((f32[2,128,2048]{2,1,0:T(8,128)}), f32[2,64,2048]{2,1,0:T(8,128)}) %reduce-scatter.5.cloned.1.call-update) | async-done | bytes 1048592 | tf_op jit(solution)/shard_map/reduce_scatter | solution.py:122
  691.7 713.3 %reduce-scatter.7.cloned.1.call-done = f32[16,1024]{1,0:T(8,128)} async-done(((f32[2048,1024]{1,0:T(8,128)}), f32[16,1024]{1,0:T(8,128)}) %reduce-scatter.7.cloned.1.call-update) | async-done | bytes 65552
  (130 shorter events, 113.9 us)
Async XLA Ops:
  7.2 112.3 %copy-start.17 = (bf16[2,64,1024]{2,1,0:T(8,128)(2,1)S(1)}, bf16[2,64,1024]{2,1,0:T(8,128)(2,1)}, u32[]{:S(2)}) copy-start(bf16[2,64,1024]{2,1,0:T(8,128)(2,1)} %param.36) | copy-start | bytes 786436
  7.2 18.5 %all-gather.2.cloned.1.call-start = ((), (), s32[]{:S(2)}) async-start(), calls=%async_computation.6 | async-start | bytes 1572864 | tf_op jit(solution)/shard_map/all_gather | solution.py:55
  27.7 85.3 %copy-start.5 = (bf16[2,128,512]{2,1,0:T(8,128)(2,1)}, bf16[2,128,512]{2,1,0:T(8,128)(2,1)S(1)}, u32[]{:S(2)}) copy-start(bf16[2,128,512]{2,1,0:T(8,128)(2,1)S(1)} %fusion.32) | copy-start | bytes 786436
  30.4 82.5 %copy-start.7 = (bf16[2,128,512]{2,1,0:T(8,128)(2,1)}, bf16[2,128,512]{2,1,0:T(8,128)(2,1)S(1)}, u32[]{:S(2)}) copy-start(bf16[2,128,512]{2,1,0:T(8,128)(2,1)S(1)} %fusion.29) | copy-start | bytes 786436
  30.5 14.7 %collective-permute-start = (bf16[2,128,1024]{2,1,0:T(8,128)(2,1)S(1)}, bf16[2,128,1024]{2,1,0:T(8,128)(2,1)S(1)}, u32[]{:S(2)}, u32[]{:S(2)}) collective-permute-start(bf16[2,128,1024]{2,1,0:T(8,128)(2,1)S(1)} %pad_maximum_fusion.2), channel_id=1, source_target_pairs={{0,2},{2,4},{4,6},{6,8},{8,10},{10,12},{12,14},{14,16},{16,18},{18... | collective-permute-start | bytes 1572872 | tf_op jit(solution)/shard_map/ppermute | solution.py:13
  45.2 15.2 %collective-permute-start.1 = (bf16[2,128,1024]{2,1,0:T(8,128)(2,1)S(1)}, bf16[2,128,1024]{2,1,0:T(8,128)(2,1)S(1)}, u32[]{:S(2)}, u32[]{:S(2)}) collective-permute-start(bf16[2,128,1024]{2,1,0:T(8,128)(2,1)S(1)} %collective-permute-done), channel_id=1, source_target_pairs={{0,2},{2,4},{4,6},{6,8},{8,10},{10,12},{12,14},{14,16},{16,18},{18... | collective-permute-start | bytes 1572872 | tf_op jit(solution)/shard_map/ppermute | solution.py:13
  60.4 14.3 %collective-permute-start.2 = (bf16[2,128,1024]{2,1,0:T(8,128)(2,1)S(1)}, bf16[2,128,1024]{2,1,0:T(8,128)(2,1)S(1)}, u32[]{:S(2)}, u32[]{:S(2)}) collective-permute-start(bf16[2,128,1024]{2,1,0:T(8,128)(2,1)S(1)} %collective-permute-done.1), channel_id=1, source_target_pairs={{0,2},{2,4},{4,6},{6,8},{8,10},{10,12},{12,14},{14,16},{16,18},{18... | collective-permute-start | bytes 1572872 | tf_op jit(solution)/shard_map/ppermute | solution.py:13
  74.7 13.4 collective-permute-start.3
  88.1 12.4 collective-permute-start.4
  100.5 12.4 collective-permute-start.5
  113.0 13.5 collective-permute-start.6
  121.0 15.7 %all-to-all-start = ((bf16[2,2,32768]{2,1,0:T(2,128)(2,1)}), bf16[2,2,32768]{2,1,0:T(2,128)(2,1)S(1)}, u32[]{:S(2)}, u32[]{:S(2)}) async-start(bf16[2,2,32768]{2,1,0:T(2,128)(2,1)} %reshape.332), calls=%async_computation | async-start | bytes 524288 | tf_op jit(solution)/shard_map/all_to_all | solution.py:58
  127.2 18.0 %collective-permute-start.7 = (bf16[1,128,1024]{2,1,0:T(8,128)(2,1)}, bf16[1,128,1024]{2,1,0:T(8,128)(2,1)}, u32[]{:S(2)}, u32[]{:S(2)}) collective-permute-start(bf16[1,128,1024]{2,1,0:T(8,128)(2,1)} %slice.224), channel_id=1, source_target_pairs={{0,2},{2,4},{4,6},{6,8},{8,10},{10,12},{12,14},{14,16},{16,18},{18... | collective-permute-start | bytes 786440 | tf_op jit(solution)/shard_map/ppermute | solution.py:13
  136.7 5.9 all-to-all-start.2
  140.9 548.7 %reduce-scatter.5.cloned.1.call-start = ((), (), s32[]{:S(2)}) async-start(), calls=%async_computation.7 | async-start | bytes 3145728 | tf_op jit(solution)/shard_map/reduce_scatter | solution.py:122
  229.2 29.8 %collective-permute-start.8 = (f32[2,128,1024]{2,1,0:T(8,128)S(1)}, f32[2,128,1024]{2,1,0:T(8,128)S(1)}, u32[]{:S(2)}, u32[]{:S(2)}) collective-permute-start(f32[2,128,1024]{2,1,0:T(8,128)S(1)} %get-tuple-element.177), channel_id=1, source_target_pairs={{2,0},{4,2},{6,4},{8,6},{10,8},{12,10},{14,12},{16,14},{18,16},{20... | collective-permute-start | bytes 3145736 | tf_op jit(solution)/shard_map/ppermute | solution.py:13
  230.8 35.1 %collective-permute-start.9 = (f32[2,128,1024]{2,1,0:T(8,128)S(1)}, f32[2,128,1024]{2,1,0:T(8,128)S(1)}, u32[]{:S(2)}, u32[]{:S(2)}) collective-permute-start(f32[2,128,1024]{2,1,0:T(8,128)S(1)} %get-tuple-element.178), channel_id=1, source_target_pairs={{4,0},{6,2},{8,4},{10,6},{12,8},{14,10},{16,12},{18,14},{20,16},{2... | collective-permute-start | bytes 3145736 | tf_op jit(solution)/shard_map/ppermute | solution.py:13
  232.1 56.1 %collective-permute-start.10 = (f32[2,128,1024]{2,1,0:T(8,128)S(1)}, f32[2,128,1024]{2,1,0:T(8,128)S(1)}, u32[]{:S(2)}, u32[]{:S(2)}) collective-permute-start(f32[2,128,1024]{2,1,0:T(8,128)S(1)} %get-tuple-element.179), channel_id=1, source_target_pairs={{6,0},{8,2},{10,4},{12,6},{14,8},{16,10},{18,12},{20,14},{22,16},{... | collective-permute-start | bytes 3145736 | tf_op jit(solution)/shard_map/ppermute | solution.py:13
  233.4 56.1 %collective-permute-start.11 = (f32[2,128,1024]{2,1,0:T(8,128)S(1)}, f32[2,128,1024]{2,1,0:T(8,128)S(1)}, u32[]{:S(2)}, u32[]{:S(2)}) collective-permute-start(f32[2,128,1024]{2,1,0:T(8,128)S(1)} %get-tuple-element.180), channel_id=1, source_target_pairs={{8,0},{10,2},{12,4},{14,6},{16,8},{18,10},{20,12},{22,14},{24,16},... | collective-permute-start | bytes 3145736 | tf_op jit(solution)/shard_map/ppermute | solution.py:13
  234.7 155.1 %collective-permute-start.12 = (f32[2,128,1024]{2,1,0:T(8,128)S(1)}, f32[2,128,1024]{2,1,0:T(8,128)S(1)}, u32[]{:S(2)}, u32[]{:S(2)}) collective-permute-start(f32[2,128,1024]{2,1,0:T(8,128)S(1)} %get-tuple-element.181), channel_id=1, source_target_pairs={{10,0},{12,2},{14,4},{16,6},{18,8},{20,10},{22,12},{24,14},{26,16}... | collective-permute-start | bytes 3145736 | tf_op jit(solution)/shard_map/ppermute | solution.py:13
  259.0 130.7 %collective-permute-start.13 = (f32[2,128,1024]{2,1,0:T(8,128)S(1)}, f32[2,128,1024]{2,1,0:T(8,128)S(1)}, u32[]{:S(2)}, u32[]{:S(2)}) collective-permute-start(f32[2,128,1024]{2,1,0:T(8,128)S(1)} %get-tuple-element.182), channel_id=1, source_target_pairs={{12,0},{14,2},{16,4},{18,6},{20,8},{22,10},{24,12},{26,14},{28,16}... | collective-permute-start | bytes 3145736 | tf_op jit(solution)/shard_map/ppermute | solution.py:13
  265.8 123.9 %collective-permute-start.14 = (f32[2,128,1024]{2,1,0:T(8,128)S(1)}, f32[2,128,1024]{2,1,0:T(8,128)S(1)}, u32[]{:S(2)}, u32[]{:S(2)}) collective-permute-start(f32[2,128,1024]{2,1,0:T(8,128)S(1)} %get-tuple-element.183), channel_id=1, source_target_pairs={{14,0},{16,2},{18,4},{20,6},{22,8},{24,10},{26,12},{28,14},{30,16}... | collective-permute-start | bytes 3145736 | tf_op jit(solution)/shard_map/ppermute | solution.py:13
  288.2 102.6 %collective-permute-start.15 = (f32[1,128,1024]{2,1,0:T(8,128)S(1)}, f32[1,128,1024]{2,1,0:T(8,128)S(1)}, u32[]{:S(2)}, u32[]{:S(2)}) collective-permute-start(f32[1,128,1024]{2,1,0:T(8,128)S(1)} %pad_maximum_fusion.1), channel_id=1, source_target_pairs={{16,0},{18,2},{20,4},{22,6},{24,8},{26,10},{28,12},{30,14},{32,16}... | collective-permute-start | bytes 1572872 | tf_op jit(solution)/shard_map/ppermute | solution.py:13
  394.5 1010.5 %reduce-scatter.7.cloned.1.call-start = ((), (), s32[]{:S(2)}) async-start(), calls=%async_computation.8 | async-start | bytes 8454144
  (19 other events, 393.1 us)
Sparse Core Ops, SparseCore 0:
  9.8 15.8 all-gather.1
  394.6 294.9 reduce-scatter.4
  692.2 712.6 reduce-scatter.6
where the time goes:
time: 1410 us
  waiting for transfers between devices  1180 us (84%)
  matrix products  77.1 us (5%)
  local copies, waits for them, and re-layouts  63.9 us (5%)
  starting transfers between devices  58.8 us (4%)
  between operations  14.3 us (1%)
    unnamed x4, waiting for transfers between devices  714 us
    reduce_scatter x1, waiting for transfers between devices, shards(): lax.psum_scatter(partial_features, 'space', scatter_dimension=1, tiled=True)  239 us
    ppermute x16, waiting for transfers between devices, passed_along(): lax.ppermute(value, axis, [(source, source + steps) for source in range(i...  207 us
    ppermute x16, starting transfers between devices, passed_along(): lax.ppermute(value, axis, [(source, source + steps) for source in range(i...  51.1 us
  transfers between devices with their start and end apart: 21, of which 14 were waited for; matrix products, arithmetic and copies ran while one was open for 4% of the time, Pallas kernels for 0%

commit v1 on v0

v1 whole, which is shorter than its diff:
```python
import jax
import jax.numpy as jnp
from jax import lax
from jax.experimental import pallas as pl
from jax.experimental.pallas import tpu as pltpu
from jax.sharding import PartitionSpec as P

HEAD = 128
WINDOW = 16
PLANE = 16
NZ = 8
OWN = 256
HALO = 128
F32 = jnp.float32
BF16 = jnp.bfloat16
VM = pltpu.VMEM
MIB = 2**20


def mm(a, b, ca, cb):
    return lax.dot_general(a, b, (((ca,), (cb,)), ((), ())), preferred_element_type=F32)


def place():
    tm = lax.axis_index("tm")
    return tm // PLANE, tm % PLANE, lax.axis_index("space")


def remote(src, dst, ssem, rsem, tm, core):
    return pltpu.make_async_remote_copy(
        src_ref=src, dst_ref=dst, send_sem=ssem, recv_sem=rsem,
        device_id=(tm, core), device_id_type=pl.DeviceIdType.MESH,
    )


def rows_at(ref, start, count):
    return ref.at[pl.ds(pl.multiple_of(start, 16), count)]


def signal(sem, tm, core):
    pl.semaphore_signal(
        sem, inc=1, device_id=(tm, core), device_id_type=pl.DeviceIdType.MESH
    )


def await_bytes(ref, sem):
    pltpu.make_async_copy(ref, ref, sem).wait()


class Sends:
    def __init__(self, sems):
        self.sems, self.used, self.waits = sems, 0, []

    def start(self, src, dst, rsem, tm, core, self_if=None):
        copy = remote(src, dst, self.sems.at[self.used], rsem, tm, core)
        self.used += 1
        if self_if is None:
            copy.start()
        else:
            pl.when(self_if)(lambda: pltpu.make_async_copy(src, dst, rsem).start())
            pl.when(jnp.logical_not(self_if))(copy.start)
        self.waits.append((copy, self_if))

    def finish(self):
        for copy, self_if in self.waits:
            if self_if is None:
                copy.wait_send()
            else:
                pl.when(jnp.logical_not(self_if))(copy.wait_send)


def exchange_kernel(f_ref, qc_ref, rows_ref, qco_ref, send, got):
    z, c, s = place()
    base = z * PLANE
    nxt = ((z + 1) % NZ) * PLANE + c
    prv = ((z + NZ - 1) % NZ) * PLANE + c
    mine = c % 2 == s
    barrier = pltpu.get_barrier_semaphore()
    for r in range(1, PLANE):
        signal(barrier, base + (c + r) % PLANE, c % 2)
    signal(barrier, base + c, 1 - s)
    signal(barrier, prv, s)
    pl.semaphore_wait(barrier, jnp.where(mine, 16, 18))

    sends = Sends(send)
    to = (c // 4) % 2
    for r in range(8):
        j = (c // 2 + r) % 8
        d = 2 * j + s
        sends.start(
            rows_at(f_ref, 16 * j, 16), rows_at(rows_ref, HALO + 16 * c, 16),
            got.at[c // 8], base + d, to, (mine & (to == s)) if r == 0 else None,
        )
    for r in range(8):
        j = (c // 2 + r) % 8
        d = 2 * j + s
        for o in range(2):
            core = (s + o) % 2
            sends.start(
                rows_at(qc_ref.at[core], 16 * j, 16), rows_at(qco_ref, 16 * c, 16),
                got.at[2], base + d, core, mine if r == 0 and o == 0 else None,
            )
    late = rows_at(rows_ref, HALO + 128 + 64 * s, 64)
    await_bytes(late, got.at[1])
    halo_there = rows_at(rows_ref, 64 * s, 64)
    sends.start(late, halo_there, got.at[3], nxt, s)
    sends.start(late, late, got.at[5], base + c, 1 - s)
    early = rows_at(rows_ref, HALO + 64 * s, 64)
    await_bytes(early, got.at[0])
    sends.start(early, early, got.at[4], base + c, 1 - s)
    await_bytes(halo_there, got.at[3])
    sends.start(halo_there, halo_there, got.at[6], base + c, 1 - s)
    await_bytes(qco_ref, got.at[2])
    await_bytes(rows_at(rows_ref, HALO + 64 * (1 - s), 64), got.at[4])
    await_bytes(rows_at(rows_ref, HALO + 128 + 64 * (1 - s), 64), got.at[5])
    await_bytes(rows_at(rows_ref, 64 * (1 - s), 64), got.at[6])
    sends.finish()


def exchange(f, qc):
    d, width = f.shape[1], qc.shape[2]
    return pl.pallas_call(
        exchange_kernel,
        out_shape=(
            jax.ShapeDtypeStruct((HALO + OWN, d), BF16),
            jax.ShapeDtypeStruct((OWN, width), BF16),
        ),
        in_specs=[pl.BlockSpec(memory_space=VM)] * 2,
        out_specs=[pl.BlockSpec(memory_space=VM)] * 2,
        scratch_shapes=[pltpu.SemaphoreType.DMA((28,)), pltpu.SemaphoreType.DMA((7,))],
        compiler_params=pltpu.CompilerParams(
            collective_id=0, has_side_effects=True, vmem_limit_bytes=16 * MIB
        ),
    )(f, qc)


def local_kernel(
    rows_ref, qc_ref, kw_ref, vw_ref, ag_ref, gf_ref, wa_ref, wb_ref, wc_ref,
    k_scr, v_scr, g_scr, acc_scr
):
    z, _, _ = place()
    half = kw_ref.shape[1]
    scale = HEAD ** -0.5
    n = OWN // 2
    k_scr[...] = mm(rows_ref[...], kw_ref[...], 1, 0).astype(BF16)
    v_scr[...] = mm(rows_ref[...], vw_ref[...], 1, 0).astype(BF16)
    acc_scr[...] = jnp.zeros_like(acc_scr)
    back = (
        lax.broadcasted_iota(jnp.int32, (n, 2 * n), 0) + HALO
        - lax.broadcasted_iota(jnp.int32, (n, 2 * n), 1)
    )
    window = (back >= 0) & (back < 8 * WINDOW) & (back % 8 == 0)
    halo_key = lax.broadcasted_iota(jnp.int32, (n, 2 * n), 1) < HALO
    for tile in range(2):
        lo = tile * n
        allowed = window & ((z > 0) | jnp.logical_not(halo_key)) if tile == 0 else window
        for h in range(half // HEAD):
            cols = slice(h * HEAD, (h + 1) * HEAD)
            vcols = slice(half + h * HEAD, half + (h + 1) * HEAD)
            q = qc_ref[lo : lo + n, cols]
            c = qc_ref[lo : lo + n, vcols]
            k = k_scr[lo : lo + 2 * n, cols]
            v = v_scr[lo : lo + 2 * n, cols]
            scores = jnp.where(allowed, mm(q, k, 1, 1) * scale, -jnp.inf)
            top = jnp.max(scores, axis=-1, keepdims=True)
            total = jnp.log(jnp.sum(jnp.exp(scores - top), axis=-1, keepdims=True)) + top
            w = jnp.exp(scores - total)
            rounded = w.astype(BF16)
            dp = mm(c, v, 1, 1)
            spread = jnp.sum(w * dp, axis=-1, keepdims=True)
            ds = (w * (dp - spread) * scale).astype(BF16)
            ag_ref[lo : lo + n, cols] = mm(rounded, v, 1, 0).astype(BF16)
            ag_ref[lo : lo + n, vcols] = mm(ds, k, 1, 0).astype(BF16)
            acc_scr[lo : lo + 2 * n, cols] += mm(ds, q, 0, 0)
            acc_scr[lo : lo + 2 * n, vcols] += mm(rounded, c, 0, 0)
    g_scr[...] = acc_scr[...].astype(BF16)
    at = 0
    for ref in (wa_ref, wb_ref, wc_ref):
        w = ref.shape[1]
        ref[...] = mm(rows_ref[...], g_scr[:, at : at + w], 0, 0).astype(BF16)
        at += w
    gf = mm(g_scr[:, :half], kw_ref[...], 1, 1) + mm(g_scr[:, half:], vw_ref[...], 1, 1)
    gf_ref[...] = gf.astype(BF16)


PARTS = (384, 384, 256)


def local(rows, qc, kw, vw):
    n_all, d = rows.shape
    n_own, width = qc.shape
    half = width // 2
    return pl.pallas_call(
        local_kernel,
        out_shape=(
            jax.ShapeDtypeStruct((n_own, width), BF16),
            jax.ShapeDtypeStruct((n_all, d), BF16),
        ) + tuple(jax.ShapeDtypeStruct((d, w), BF16) for w in PARTS),
        in_specs=[pl.BlockSpec(memory_space=VM)] * 4,
        out_specs=[pl.BlockSpec(memory_space=VM)] * 5,
        scratch_shapes=[
            pltpu.VMEM((n_all, half), BF16),
            pltpu.VMEM((n_all, half), BF16),
            pltpu.VMEM((n_all, width), BF16),
            pltpu.VMEM((n_all, width), F32),
        ],
        compiler_params=pltpu.CompilerParams(vmem_limit_bytes=48 * MIB),
    )(rows, qc, kw, vw)


class Ring4:
    def __init__(self, sends, view, up, down, bufs, sems, out):
        self.sends, self.view, self.up, self.down = sends, view, up, down
        self.bufs, self.sems, self.out = bufs, sems, out

    def first(self):
        from_below, from_above, below, above = self.bufs
        h = below.shape[0] // 2
        self.sends.start(self.view(2, 0), from_below, self.sems.at[0], *self.up)
        self.sends.start(self.view(2, 1), from_above, self.sems.at[1], *self.down)
        self.sends.start(self.view(1, 1), below.at[pl.ds(h, h)], self.sems.at[2], *self.up)
        self.sends.start(self.view(3, 0), above.at[pl.ds(0, h)], self.sems.at[3], *self.down)

    def second(self):
        from_below, from_above, below, above = self.bufs
        h = below.shape[0] // 2
        for buf, sem, view, dst, dsem, dev in (
            (from_below, 0, self.view(1, 0), below.at[pl.ds(0, h)], 4, self.up),
            (from_above, 1, self.view(3, 1), above.at[pl.ds(h, h)], 5, self.down),
        ):
            await_bytes(buf, self.sems.at[sem])

            def add(i, _):
                buf[i] = (buf[i].astype(F32) + view[i].astype(F32)).astype(BF16)
                return 0

            lax.fori_loop(0, h, add, 0)
            self.sends.start(buf, dst, self.sems.at[dsem], *dev)

    def third(self):
        from_below, from_above, below, above = self.bufs
        h = below.shape[0] // 2
        await_bytes(below.at[pl.ds(h, h)], self.sems.at[2])
        await_bytes(above.at[pl.ds(0, h)], self.sems.at[3])
        await_bytes(below.at[pl.ds(0, h)], self.sems.at[4])
        await_bytes(above.at[pl.ds(h, h)], self.sems.at[5])
        for half in range(2):
            own = self.view(0, half)

            def add(i, _):
                j = half * h + i
                self.out[j] = (
                    own[i].astype(F32) + below[j].astype(F32) + above[j].astype(F32)
                ).astype(BF16)
                return 0

            lax.fori_loop(0, h, add, 0)


def return_kernel(
    ag_ref, gf_ref, wa_ref, wb_ref, wc_ref, rag_ref, rgf_ref, gk_ref, gv_ref,
    gx, gh, a1, a2, a3, a4, ra, a5, a6, a7, a8, ra2, za,
    b1, b2, b3, b4, rb, b5, b6, b7, b8, rb2, zb, cb, rc, cc,
    send, gsem, a1sem, a2sem, b1sem, b2sem, csem, fsem
):
    z, c, s = place()
    y, x = c // 4, c % 4
    base = z * PLANE
    prv = ((z + NZ - 1) % NZ) * PLANE + c
    nxt = ((z + 1) % NZ) * PLANE + c
    barrier = pltpu.get_barrier_semaphore()
    for r in range(1, PLANE):
        for core in range(2):
            signal(barrier, base + (c + r) % PLANE, core)
    signal(barrier, base + c, 1 - s)
    for r in range(1, NZ):
        signal(barrier, ((z + r) % NZ) * PLANE + c, s)
    pl.semaphore_wait(barrier, 2 * (PLANE - 1) + 1 + NZ - 1)

    sends = Sends(send)
    home = c % 2
    slot = 16 * (c // 2)
    for r in range(PLANE):
        d = (c + r) % PLANE
        sends.start(
            rows_at(ag_ref, 16 * d, 16), rows_at(rag_ref.at[s], slot, 16),
            gsem.at[0], base + d, home, (home == s) if r == 0 else None,
        )
    for i in range(3):
        sends.start(
            rows_at(gf_ref, 128 * i + 64 * (1 - s), 64), gx.at[pl.ds(64 * i, 64)],
            gsem.at[1 + i], base + c, 1 - s,
        )

    def tm_x(v):
        return base + y * 4 + v

    def tm_y(v):
        return base + v * 4 + x

    xi = [(x + r) % 4 for r in range(4)]
    yi = [(y + r) % 4 for r in range(4)]
    zi = [(z + r) % NZ for r in range(NZ)]
    ring_a1 = Ring4(
        sends, lambda r, h: wa_ref.at[pl.ds(4 * h, 4), :, xi[r]],
        (tm_x(xi[1]), s), (tm_x(xi[3]), s), (a1, a2, a3, a4), a1sem, ra,
    )
    ring_b1 = Ring4(
        sends, lambda r, h: wb_ref.at[pl.ds(4 * h, 4), yi[r]],
        (tm_y(yi[1]), s), (tm_y(yi[3]), s), (b1, b2, b3, b4), b1sem, rb,
    )
    ring_a2 = Ring4(
        sends, lambda r, h: ra.at[pl.ds(4 * h, 4), yi[r]],
        (tm_y(yi[1]), s), (tm_y(yi[3]), s), (a5, a6, a7, a8), a2sem, ra2,
    )
    ring_b2 = Ring4(
        sends, lambda r, h: rb.at[pl.ds(4 * h, 4), xi[r]],
        (tm_x(xi[1]), s), (tm_x(xi[3]), s), (b5, b6, b7, b8), b2sem, rb2,
    )
    chains = ((1, 0, 4, 0), (-1, 1, 4, 4), (1, 1, 3, 8), (-1, 0, 3, 11))

    def c_view(rel, h):
        return wc_ref.at[zi[rel % NZ], pl.ds(2 * h, 2)]

    def c_step(k):
        for way, h, length, first in chains:
            if k >= length:
                continue
            dev = (nxt if way == 1 else prv, s)
            own = c_view(way * (length - k), h)
            if k == 0:
                src = own
            else:
                src = cb.at[first + k - 1]
                await_bytes(src, csem.at[first + k - 1])

                def add(i, _):
                    src[i] = (src[i].astype(F32) + own[i].astype(F32)).astype(BF16)
                    return 0

                lax.fori_loop(0, 2, add, 0)
            sends.start(src, cb.at[first + k], csem.at[first + k], *dev)

    ring_a1.first()
    ring_b1.first()
    c_step(0)

    def add_gf(i):
        await_bytes(gx.at[pl.ds(64 * i, 64)], gsem.at[1 + i])

        def add(t, _):
            there = pl.ds(pl.multiple_of(64 * i + 16 * t, 16), 16)
            here = pl.ds(pl.multiple_of(128 * i + 64 * s + 16 * t, 16), 16)
            gx[there] = (gx[there].astype(F32) + gf_ref[here].astype(F32)).astype(BF16)
            return 0

        lax.fori_loop(0, 4, add, 0)

    def gf_home(i):
        for r in range(4):
            t = (c + r) % 4
            d = 8 * (i - 1) + 4 * s + t
            sends.start(
                rows_at(gx, 64 * i + 16 * t, 16), rows_at(rgf_ref, slot, 16),
                gsem.at[5], base + d, home, ((d == c) & (home == s)) if r == 0 else None,
            )

    add_gf(0)
    sends.start(gx.at[pl.ds(0, 64)], gh, gsem.at[4], prv, s)
    add_gf(1)
    gf_home(1)
    add_gf(2)
    c_step(1)
    await_bytes(gh, gsem.at[4])

    def add_halo(t, _):
        there = pl.ds(pl.multiple_of(128 + 16 * t, 16), 16)
        here = pl.ds(pl.multiple_of(16 * t, 16), 16)
        gx[there] = (gx[there].astype(F32) + gh[here].astype(F32)).astype(BF16)
        return 0

    lax.fori_loop(0, 4, add_halo, 0)
    gf_home(2)
    ring_a1.second()
    ring_b1.second()
    c_step(2)
    ring_a1.third()
    ring_a2.first()
    ring_b1.third()
    ring_b2.first()
    c_step(3)
    ring_a2.second()
    ring_b2.second()
    for way, h, length, first in chains:
        await_bytes(cb.at[first + length - 1], csem.at[first + length - 1])
    for h, (p, m) in enumerate(((0, 3), (2, 1))):
        fp, fm = (chains[t][3] + chains[t][2] - 1 for t in (p, m))
        own = c_view(0, h)

        def add(i, _):
            rc[2 * h + i] = (
                own[i].astype(F32) + cb[fp, i].astype(F32) + cb[fm, i].astype(F32)
            ).astype(BF16)
            return 0

        lax.fori_loop(0, 2, add, 0)
    for r in range(1, PLANE):
        yy, xx = yi[r // 4], xi[r % 4]
        sends.start(rc.at[yy, xx], cc.at[r - 1], fsem.at[0], base + yy * 4 + xx, s)
    for ring, out, buf, sem in ((ring_a2, ra2, za, fsem.at[1]), (ring_b2, rb2, zb, fsem.at[2])):
        ring.third()
        for r in range(1, NZ):
            sends.start(out.at[zi[r]], buf.at[r - 1], sem, zi[r] * PLANE + c, s)

    def total(own, buf, count):
        return lax.fori_loop(
            0, count, lambda i, acc: acc + buf[i].astype(F32), own.astype(F32)
        )

    await_bytes(cc, fsem.at[0])
    gv_ref[:, 256:512] = total(rc[y, x], cc, PLANE - 1)
    await_bytes(za, fsem.at[1])
    gk_ref[:, 0:384] = total(ra2[z], za, NZ - 1)
    await_bytes(zb, fsem.at[2])
    last = total(rb2[z], zb, NZ - 1)
    gk_ref[:, 384:512] = last[:, :128]
    gv_ref[:, 0:256] = last[:, 128:]
    await_bytes(rag_ref, gsem.at[0])
    await_bytes(rgf_ref, gsem.at[5])
    sends.finish()


def give_back(ag, gf, wa, wb, wc):
    d = gf.shape[1]
    width = ag.shape[1]
    a, b, cw = PARTS

    def ring(w, mid):
        lead = (4, 4) if mid else (4,)
        full = (8, 4) if mid else (8,)
        return [pltpu.VMEM(lead + (16, w), BF16)] * 2 + [pltpu.VMEM(full + (16, w), BF16)] * 3

    sem = pltpu.SemaphoreType.DMA
    return pl.pallas_call(
        return_kernel,
        out_shape=(
            jax.ShapeDtypeStruct((2, 128, width), BF16),
            jax.ShapeDtypeStruct((128, d), BF16),
            jax.ShapeDtypeStruct((16, width // 2), F32),
            jax.ShapeDtypeStruct((16, width // 2), F32),
        ),
        in_specs=[pl.BlockSpec(memory_space=VM)] * 5,
        out_specs=[pl.BlockSpec(memory_space=VM)] * 4,
        scratch_shapes=[pltpu.VMEM((192, d), BF16), pltpu.VMEM((64, d), BF16)]
        + ring(a, True) + ring(a, False) + [pltpu.VMEM((7, 16, a), BF16)]
        + ring(b, True) + ring(b, False) + [pltpu.VMEM((7, 16, b), BF16)]
        + [
            pltpu.VMEM((14, 2, 4, 16, cw), BF16),
            pltpu.VMEM((4, 4, 16, cw), BF16),
            pltpu.VMEM((15, 16, cw), BF16),
            sem((128,)), sem((6,)), sem((6,)), sem((6,)), sem((6,)), sem((6,)), sem((14,)),
            sem((3,)),
        ],
        compiler_params=pltpu.CompilerParams(
            collective_id=1, has_side_effects=True, vmem_limit_bytes=48 * MIB
        ),
    )(ag, gf, *(w.reshape(8, 4, 4, 16, w.shape[1]) for w in (wa, wb, wc)))


def shards(features, queries, cotangent, key_weight, value_weight):
    frames, patches, d = features.shape
    half = key_weight.shape[1]

    def split(v):
        w = v.shape[2]
        return v.reshape(frames, 8, 8, w).transpose(1, 0, 2, 3).reshape(128, w)

    def join(v):
        w = v.shape[1]
        return v.reshape(8, frames, 8, w).transpose(1, 0, 2, 3).reshape(frames, patches, w)

    f, q, c = split(features), split(queries), split(cotangent)
    qc = jnp.stack(
        [jnp.concatenate([q[:, at : at + half], c[:, at : at + half]], axis=1) for at in (0, half)]
    )
    rows, qc = exchange(f, qc)
    ag, gf, wa, wb, wc = local(rows, qc, key_weight, value_weight)
    ag, gf, gk, gv = give_back(ag, gf, wa, wb, wc)
    att = join(jnp.concatenate([ag[0, :, :half], ag[1, :, :half]], axis=1))
    gq = join(jnp.concatenate([ag[0, :, half:], ag[1, :, half:]], axis=1))
    return att, join(gf), gq, gk, gv


def solution(mesh):
    rows = P("tm", "space", None)
    return jax.shard_map(
        shards,
        mesh=mesh,
        in_specs=(rows, rows, rows, P(None, "space"), P(None, "space")),
        out_specs=(rows, rows, rows, P("tm", "space"), P("tm", "space")),
        check_vma=False,
    )
```

time: 1410 us -> 94.1 us (0.07)
  the two profiles are of different devices: /device:TPU:0 before, /device:TPU:32 now
where the time goes in v1:
time: 94.1 us; the launch traced here: 93 us
  Pallas kernels  85.4 us (91%)
  local copies, waits for them, and re-layouts  5.33 us (6%)
  other arithmetic  1.57 us (2%)
    pallas_call x1, Pallas kernels, give_back(): pl.pallas_call(return_kernel, out_shape=(jax.ShapeDtypeStruct((2, 128, wi...  52.3 us
    pallas_call x1, Pallas kernels, exchange(): pl.pallas_call(exchange_kernel, out_shape=(jax.ShapeDtypeStruct((HALO + O...  20.3 us
    pallas_call x1, Pallas kernels, local(): pl.pallas_call(local_kernel, out_shape=(jax.ShapeDtypeStruct((n_own, widt...  12.8 us
    unnamed x6, local copies, waits for them, and re-layouts  2.38 us
    reshape x3, local copies, waits for them, and re-layouts, split(): return v.reshape(frames, 8, 8, w).transpose(1, 0, 2, 3).reshape(128, w)  2.03 us

profile of v1, /device:TPU:32, one launch (start us, length us, event | category | flops | bytes accessed | tf_op | source)
XLA Modules:
  0.0 93.0 jit_solution(1998789141409872419)
XLA Ops:
  0.6 1.0 %copy.11 = bf16[2,8,8,1024]{3,2,0,1:T(8,128)(2,1)S(1)} copy(bf16[2,8,8,1024]{3,2,1,0:T(8,128)(2,1)} %bitcast.52) | data formatting | bytes 524288 | tf_op jit(solution)/shard_map/reshape | solution.py:476
  1.6 0.0 copy-start.1
  1.6 1.0 %copy.12 = bf16[2,8,8,1024]{3,2,0,1:T(8,128)(2,1)S(1)} copy(bf16[2,8,8,1024]{3,2,1,0:T(8,128)(2,1)} %bitcast.53) | data formatting | bytes 524288 | tf_op jit(solution)/shard_map/reshape | solution.py:476
  2.7 0.1 maximum_bitcast_fusion
  2.8 0.1 pad_maximum_fusion.qc_ref
  2.8 0.0 copy-done.1
  2.9 20.3 %shard_map.92 = (bf16[384,2048]{1,0:T(8,128)(2,1)S(1)}, bf16[256,1024]{1,0:T(8,128)(2,1)S(1)}) custom-call(bf16[128,2048]{1,0:T(8,128)(2,1)S(1)} %bitcast.39, bf16[2,128,1024]{2,1,0:T(8,128)(2,1)S(1)} %pad_maximum_fusion.qc_ref), custom_call_target="tpu_custom_call" | custom-call | tf_op jit(solution)/shard_map/pallas_call | solution.py:122
  23.1 0.0 copy-start
  23.2 1.1 %copy-done = bf16[384,2048]{1,0:T(8,128)(2,1)} copy-done((bf16[384,2048]{1,0:T(8,128)(2,1)}, bf16[384,2048]{1,0:T(8,128)(2,1)S(1)}, u32[]{:S(2)}) %copy-start) | copy-done | bytes 1572888
  24.3 12.8 %shard_map.93 = (bf16[256,1024]{1,0:T(8,128)(2,1)S(1)}, bf16[384,2048]{1,0:T(8,128)(2,1)S(1)}, bf16[2048,384]{1,0:T(8,128)(2,1)S(1)}, bf16[2048,384]{1,0:T(8,128)(2,1)}, bf16[2048,256]{1,0:T(8,128)(2,1)S(1)}) custom-call(bf16[384,2048]{1,0:T(8,128)(2,1)} %copy-done, bf16[256,1024]{1,0:T(8,128)(2,1)S(1)} %get-tuple-element.17.qc_ref, ...), custom_call_target="tpu_custom_call" | custom-call | tf_op jit(solution)/shard_map/pallas_call | solution.py:193
  37.1 52.3 %shard_map.94 = (bf16[2,128,1024]{2,1,0:T(8,128)(2,1)S(1)}, bf16[128,2048]{1,0:T(8,128)(2,1)S(1)}, f32[16,512]{1,0:T(8,128)S(1)}, f32[16,512]{1,0:T(8,128)S(1)}) custom-call(bf16[256,1024]{1,0:T(8,128)(2,1)S(1)} %get-tuple-element.18.ag_ref, bf16[384,2048]{1,0:T(8,128)(2,1)S(1)} %get-tuple-element.19.gf_ref, bf16[8,4,4,16,384]{4,3,2,1,0:T(8,128)(2,1)S(1)} %bitcast.40, ...), custom_call_target="tpu_custom_call" | custom-call | tf_op jit(solution)/shard_map/pallas_call | solution.py:444
  89.4 0.8 copy.19
  90.3 0.7 copy_bitcast_fusion.1
  91.0 0.7 copy_bitcast_fusion.2
  91.8 0.6 copy.22
  92.4 0.6 copy.23
  (4 shorter events, 0.1 us)
Async XLA Ops:
  1.6 1.2 %copy-start.1 = (bf16[2,64,2048]{2,1,0:T(8,128)(2,1)S(1)}, bf16[2,64,2048]{2,1,0:T(8,128)(2,1)}, u32[]{:S(2)}) copy-start(bf16[2,64,2048]{2,1,0:T(8,128)(2,1)} %param.5) | copy-start | bytes 1572868
  23.1 1.1 %copy-start = (bf16[384,2048]{1,0:T(8,128)(2,1)}, bf16[384,2048]{1,0:T(8,128)(2,1)S(1)}, u32[]{:S(2)}) copy-start(bf16[384,2048]{1,0:T(8,128)(2,1)S(1)} %get-tuple-element.16.rows_ref) | copy-start | bytes 4718596

commit v2 on v0

v2 whole, which is shorter than its diff:
```python
import jax
import jax.numpy as jnp
from jax import lax
from jax.experimental import pallas as pl
from jax.experimental.pallas import tpu as pltpu
from jax.sharding import PartitionSpec as P

HEAD = 128
WINDOW = 16
PLANE = 16
NZ = 8
OWN = 256
HALO = 128
ALL = HALO + OWN
HALF = 512
D = 2048
F32 = jnp.float32
BF16 = jnp.bfloat16
MIB = 2**20


def mm(a, b, ca, cb):
    return lax.dot_general(a, b, (((ca,), (cb,)), ((), ())), preferred_element_type=F32)


def rows_at(ref, start, count):
    return ref.at[pl.ds(pl.multiple_of(start, 16), count)]


def signal(sem, tm, core):
    pl.semaphore_signal(
        sem, inc=1, device_id=(tm, core), device_id_type=pl.DeviceIdType.MESH
    )


def await_bytes(ref, sem):
    pltpu.make_async_copy(ref, ref, sem).wait()


class Sends:
    def __init__(self, sems):
        self.sems, self.used, self.waits = sems, 0, []

    def start(self, src, dst, rsem, tm, core, self_if=None):
        copy = pltpu.make_async_remote_copy(
            src_ref=src, dst_ref=dst, send_sem=self.sems.at[self.used], recv_sem=rsem,
            device_id=(tm, core), device_id_type=pl.DeviceIdType.MESH,
        )
        self.used += 1
        if self_if is None:
            copy.start()
        else:
            pl.when(self_if)(lambda: pltpu.make_async_copy(src, dst, rsem).start())
            pl.when(jnp.logical_not(self_if))(copy.start)
        self.waits.append((copy, self_if))

    def finish(self):
        for copy, self_if in self.waits:
            if self_if is None:
                copy.wait_send()
            else:
                pl.when(jnp.logical_not(self_if))(copy.wait_send)


class Ring4:
    def __init__(self, sends, view, up, down, bufs, sems, out):
        self.sends, self.view, self.up, self.down = sends, view, up, down
        self.bufs, self.sems, self.out = bufs, sems, out

    def first(self):
        self.sends.start(self.view(2, 0), self.bufs[0], self.sems.at[0], *self.up)
        self.sends.start(self.view(2, 1), self.bufs[1], self.sems.at[1], *self.down)

    def direct(self):
        _, _, below, above = self.bufs
        h = below.shape[0] // 2
        self.sends.start(self.view(1, 1), below.at[pl.ds(h, h)], self.sems.at[2], *self.up)
        self.sends.start(self.view(3, 0), above.at[pl.ds(0, h)], self.sems.at[3], *self.down)

    def second(self):
        from_below, from_above, below, above = self.bufs
        h = below.shape[0] // 2
        for buf, sem, view, dst, dsem, dev in (
            (from_below, 0, self.view(1, 0), below.at[pl.ds(0, h)], 4, self.up),
            (from_above, 1, self.view(3, 1), above.at[pl.ds(h, h)], 5, self.down),
        ):
            await_bytes(buf, self.sems.at[sem])

            def add(i, _):
                buf[i] = (buf[i].astype(F32) + view[i].astype(F32)).astype(BF16)
                return 0

            lax.fori_loop(0, h, add, 0)
            self.sends.start(buf, dst, self.sems.at[dsem], *dev)

    def third(self):
        _, _, below, above = self.bufs
        h = below.shape[0] // 2
        await_bytes(below.at[pl.ds(h, h)], self.sems.at[2])
        await_bytes(above.at[pl.ds(0, h)], self.sems.at[3])
        await_bytes(below.at[pl.ds(0, h)], self.sems.at[4])
        await_bytes(above.at[pl.ds(h, h)], self.sems.at[5])
        for half in range(2):
            own = self.view(0, half)

            def add(i, _):
                j = half * h + i
                self.out[j] = (
                    own[i].astype(F32) + below[j].astype(F32) + above[j].astype(F32)
                ).astype(BF16)
                return 0

            lax.fori_loop(0, h, add, 0)


NQ = 2
CHAINS = ((1, 0, 4, 0), (-1, 1, 4, 4), (1, 1, 3, 8), (-1, 0, 3, 11))


def kernel(
    f_ref, q_ref, c_ref, kw_hbm, vw_hbm,
    att_out, gf_out, gq_out, gk_out, gv_out,
    kw, vw, fb, qcb, rows, qc, rt, k_scr, v_scr, acc, g, ag, gfp, rag, rgf, gx, gh,
    wa, wb, wc, ring_up, ring_down, ring_below, ring_above, plane_out,
    ring2_up, ring2_down, ring2_below, ring2_above, z_out, z_in, cb, rc, cc,
    send, wsem, got, fsem, hsem, gsem, r1sem, r2sem, csem, endsem,
):
    tm = lax.axis_index("tm")
    s = lax.axis_index("space")
    z, c = tm // PLANE, tm % PLANE
    y, x = c // 4, c % 4
    base = z * PLANE
    zi = [(z + r) % NZ for r in range(NZ)]
    yi = [(y + r) % 4 for r in range(4)]
    xi = [(x + r) % 4 for r in range(4)]
    nxt, prv = zi[1] * PLANE + c, zi[7] * PLANE + c

    weights = [
        pltpu.make_async_copy(kw_hbm, kw, wsem.at[0]),
        pltpu.make_async_copy(vw_hbm, vw, wsem.at[1]),
    ]
    for copy in weights:
        copy.start()
    barrier = pltpu.get_barrier_semaphore()
    for r in range(1, PLANE):
        for core in range(2):
            signal(barrier, base + (c + r) % PLANE, core)
    signal(barrier, base + c, 1 - s)
    for r in range(1, NZ):
        signal(barrier, zi[r] * PLANE + c, s)

    def pack(ref, out, cols, at):
        w = cols[1] - cols[0]
        for t in range(4):
            p, q = (ref[i, 16 * t : 16 * t + 16, cols[0] : cols[1]].astype(F32) for i in range(2))
            out[32 * t : 32 * t + 32, at : at + w] = jnp.concatenate(
                [p[:8], q[:8], p[8:], q[8:]], axis=0
            ).astype(BF16)

    pack(f_ref, fb, (0, D), 0)
    pl.semaphore_wait(barrier, 2 * (PLANE - 1) + 1 + NZ - 1)

    sends = Sends(send)
    to = (c // 4) % 2
    mine = c % 2 == s
    for r in range(8):
        j = (c // 2 + r) % 8
        sends.start(
            rows_at(fb, 16 * j, 16), rows_at(rows, HALO + 16 * c, 16), fsem.at[c],
            base + 2 * j + s, to, (mine & (to == s)) if r == 0 else None,
        )
    for core in range(2):
        pack(q_ref, qcb.at[core], (HALF * core, HALF * core + HALF), 0)
        pack(c_ref, qcb.at[core], (HALF * core, HALF * core + HALF), HALF)
    for r in range(4):
        i = 4 * s + xi[r]
        block = rows_at(rows, HALO + 128 + 16 * i, 16)
        await_bytes(block, fsem.at[8 + i])
        sends.start(block, rows_at(rows, 16 * i, 16), hsem.at[i], nxt, s)
        sends.start(block, block, got.at[0], base + c, 1 - s)
    for r in range(8):
        j = (c // 2 + r) % 8
        for o in range(2):
            core = (s + o) % 2
            sends.start(
                rows_at(qcb.at[core], 16 * j, 16), rows_at(qc, 16 * c, 16), got.at[3],
                base + 2 * j + s, core, mine if r == 0 and o == 0 else None,
            )
    for r in range(4):
        i = 4 * s + xi[r]
        block = rows_at(rows, HALO + 16 * i, 16)
        await_bytes(block, fsem.at[i])
        sends.start(block, block, got.at[1], base + c, 1 - s)

    def project(lo):
        part = rows[lo : lo + 128, :]
        k_scr[lo : lo + 128, :] = mm(part, kw[...], 1, 0).astype(BF16)
        v_scr[lo : lo + 128, :] = mm(part, vw[...], 1, 0).astype(BF16)
        rt[:, :, :, :, lo : lo + 128] = part.T.reshape(8, 4, 4, 16, 128)

    def other(lo):
        return rows_at(rows, lo + 64 * (1 - s), 64)

    for copy in weights:
        copy.wait()
    await_bytes(other(HALO + 128), got.at[0])
    project(HALO + 128)
    for r in range(4):
        i = 4 * s + xi[r]
        block = rows_at(rows, 16 * i, 16)
        await_bytes(block, hsem.at[i])
        sends.start(block, block, got.at[2], base + c, 1 - s)
    await_bytes(other(HALO), got.at[1])
    project(HALO)
    await_bytes(other(0), got.at[2])
    project(0)
    acc[...] = jnp.zeros_like(acc)
    await_bytes(qc, got.at[3])

    scale = HEAD ** -0.5
    n = OWN // 2
    col = lax.broadcasted_iota(jnp.int32, (n, 2 * n), 1)
    back = lax.broadcasted_iota(jnp.int32, (n, 2 * n), 0) + HALO - col
    window = (back >= 0) & (back < 8 * WINDOW) & (back % 8 == 0)
    home = c % 2
    slot = 16 * (c // 2)
    for tile in (1, 0):
        lo = tile * n
        allowed = window & ((z > 0) | (col >= HALO)) if tile == 0 else window
        for h in range(HALF // HEAD):
            cols = slice(h * HEAD, (h + 1) * HEAD)
            vcols = slice(HALF + h * HEAD, HALF + (h + 1) * HEAD)
            q = qc[lo : lo + n, cols]
            cot = qc[lo : lo + n, vcols]
            k = k_scr[lo : lo + 2 * n, cols]
            v = v_scr[lo : lo + 2 * n, cols]
            scores = jnp.where(allowed, mm(q, k, 1, 1) * scale, -jnp.inf)
            top = jnp.max(scores, axis=-1, keepdims=True)
            total = jnp.log(jnp.sum(jnp.exp(scores - top), axis=-1, keepdims=True)) + top
            w = jnp.exp(scores - total)
            rounded = w.astype(BF16)
            dp = mm(cot, v, 1, 1)
            spread = jnp.sum(w * dp, axis=-1, keepdims=True)
            ds = (w * (dp - spread) * scale).astype(BF16)
            ag[lo : lo + n, cols] = mm(rounded, v, 1, 0).astype(BF16)
            ag[lo : lo + n, vcols] = mm(ds, k, 1, 0).astype(BF16)
            acc[lo : lo + 2 * n, cols] += mm(ds, q, 0, 0)
            acc[lo : lo + 2 * n, vcols] += mm(rounded, cot, 0, 0)
        for r in range(8):
            d = 8 * tile + (c + r) % 8
            sends.start(
                rows_at(ag, 16 * d, 16), rows_at(rag.at[s], slot, 16), gsem.at[0],
                base + d, home, ((home == s) & (d == c)) if r == 0 else None,
            )
    g[...] = acc[...].astype(BF16)

    def c_view(r, h):
        return wc.at[r % NZ, pl.ds(2 * h, 2)]

    def c_make(r):
        wc[r] = mm(rt[zi[r]].reshape(256, ALL), g[:, HALF:], 1, 0).astype(BF16).reshape(
            4, 4, 16, HALF
        )

    def c_step(k):
        for way, h, length, first in CHAINS:
            if k >= length:
                continue
            own = c_view(way * (length - k), h)
            src = own
            if k > 0:
                src = cb.at[first + k - 1]
                await_bytes(src, csem.at[first + k - 1])

                def add(i, _):
                    src[i] = (src[i].astype(F32) + own[i].astype(F32)).astype(BF16)
                    return 0

                lax.fori_loop(0, 2, add, 0)
            sends.start(src, cb.at[first + k], csem.at[first + k], nxt if way == 1 else prv, s)

    def ab_make(out, r, lhs, lo):
        v = mm(lhs.reshape(512, ALL), g[:, lo : lo + 256], 1, 0).astype(BF16)
        for t in range(NQ):
            out[t, r] = v[:, 128 * t : 128 * t + 128].reshape(8, 4, 16, 128)

    up_x, down_x = (base + y * 4 + xi[1], s), (base + y * 4 + xi[3], s)
    up_y, down_y = (base + yi[1] * 4 + x, s), (base + yi[3] * 4 + x, s)
    plane_rings, line_rings = [], []
    for t in range(2 * NQ):
        part, q = t // NQ, t % NQ
        own = (wa, wb)[part].at[q]
        mid = plane_out.at[t]
        over = (yi, xi)[part]
        plane_rings.append(Ring4(
            sends, lambda r, h, own=own: own.at[r, pl.ds(4 * h, 4)],
            *((up_x, down_x), (up_y, down_y))[part],
            (ring_up.at[t], ring_down.at[t], ring_below.at[t], ring_above.at[t]),
            r1sem.at[t], mid,
        ))
        line_rings.append(Ring4(
            sends, lambda r, h, mid=mid, over=over: mid.at[pl.ds(4 * h, 4), over[r]],
            *((up_y, down_y), (up_x, down_x))[part],
            (ring2_up.at[t], ring2_down.at[t], ring2_below.at[t], ring2_above.at[t]),
            r2sem.at[t], z_out.at[t],
        ))

    def a_make(r):
        ab_make(wa, r, rt[:, :, xi[r]], 0)

    def b_make(r):
        ab_make(wb, r, rt[:, yi[r]], 256)

    for r in (4, 3, 5):
        c_make(r)
    c_step(0)
    a_make(2)
    plane_rings[0].first()
    b_make(2)
    plane_rings[2].first()
    plane_rings[1].first()
    plane_rings[3].first()
    a_make(1)
    a_make(3)
    plane_rings[0].direct()
    b_make(1)
    b_make(3)
    plane_rings[2].direct()
    plane_rings[1].direct()
    plane_rings[3].direct()
    for r in (2, 6, 1, 7, 0):
        c_make(r)
    a_make(0)
    b_make(0)

    def gf_make(lo, count):
        gfp[lo : lo + count, :] = (
            mm(g[lo : lo + count, :HALF], kw[...], 1, 1)
            + mm(g[lo : lo + count, HALF:], vw[...], 1, 1)
        ).astype(BF16)

    def gf_cross(i):
        sends.start(
            rows_at(gfp, 128 * i + 64 * (1 - s), 64), gx.at[pl.ds(64 * i, 64)],
            gsem.at[1 + i], base + c, 1 - s,
        )

    def gf_add(i):
        await_bytes(gx.at[pl.ds(64 * i, 64)], gsem.at[1 + i])

        def add(t, _):
            there = pl.ds(pl.multiple_of(64 * i + 16 * t, 16), 16)
            here = pl.ds(pl.multiple_of(128 * i + 64 * s + 16 * t, 16), 16)
            gx[there] = (gx[there].astype(F32) + gfp[here].astype(F32)).astype(BF16)
            return 0

        lax.fori_loop(0, 4, add, 0)

    def gf_home(i):
        for r in range(4):
            t = (c + r) % 4
            d = 8 * (i - 1) + 4 * s + t
            sends.start(
                rows_at(gx, 64 * i + 16 * t, 16), rows_at(rgf, slot, 16), gsem.at[5],
                base + d, home, ((d == c) & (home == s)) if r == 0 else None,
            )

    gf_make(0, HALO)
    gf_cross(0)
    gf_make(HALO, OWN)
    gf_cross(1)
    gf_cross(2)
    gf_add(0)
    sends.start(gx.at[pl.ds(0, 64)], gh, gsem.at[4], prv, s)
    c_step(1)
    for t in (0, 2, 1, 3):
        plane_rings[t].second()
    gf_add(1)
    gf_home(1)
    gf_add(2)
    c_step(2)
    await_bytes(gh, gsem.at[4])

    def add_halo(t, _):
        there = pl.ds(pl.multiple_of(128 + 16 * t, 16), 16)
        here = pl.ds(pl.multiple_of(16 * t, 16), 16)
        gx[there] = (gx[there].astype(F32) + gh[here].astype(F32)).astype(BF16)
        return 0

    lax.fori_loop(0, 4, add_halo, 0)
    gf_home(2)
    for t in (0, 2, 1, 3):
        plane_rings[t].third()
        line_rings[t].first()
        line_rings[t].direct()
    c_step(3)
    for t in (0, 2, 1, 3):
        line_rings[t].second()
    for t in (0, 2, 1, 3):
        line_rings[t].third()
    for r in range(1, NZ):
        sends.start(z_out.at[:, zi[r]], z_in.at[r - 1], endsem.at[0], zi[r] * PLANE + c, s)
    for way, h, length, first in CHAINS:
        await_bytes(cb.at[first + length - 1], csem.at[first + length - 1])
    for h, (p, m) in enumerate(((3, 13), (10, 7))):
        own = c_view(0, h)

        def add(i, _):
            rc[2 * h + i] = (
                own[i].astype(F32) + cb[p, i].astype(F32) + cb[m, i].astype(F32)
            ).astype(BF16)
            return 0

        lax.fori_loop(0, 2, add, 0)
    for r in range(1, PLANE):
        yy, xx = yi[r // 4], xi[r % 4]
        sends.start(rc.at[yy, xx], cc.at[r - 1], endsem.at[1], base + yy * 4 + xx, s)

    def unpack(value):
        v = value.astype(F32)
        return (
            jnp.concatenate([v[0:8], v[16:24]], axis=0).astype(BF16),
            jnp.concatenate([v[8:16], v[24:32]], axis=0).astype(BF16),
        )

    await_bytes(rag, gsem.at[0])
    for core in range(2):
        for out, at in ((att_out, 0), (gq_out, HALF)):
            for t in range(4):
                for fr, v in enumerate(unpack(rag[core, 32 * t : 32 * t + 32, at : at + HALF])):
                    out[fr, 16 * t : 16 * t + 16, HALF * core : HALF * core + HALF] = v
    await_bytes(rgf, gsem.at[5])
    for t in range(4):
        for fr, v in enumerate(unpack(rgf[32 * t : 32 * t + 32, :])):
            gf_out[fr, 16 * t : 16 * t + 16, :] = v

    await_bytes(z_in, endsem.at[0])
    for t in range(2 * NQ):
        gk_out[:, 128 * t : 128 * t + 128] = lax.fori_loop(
            0, NZ - 1, lambda i, v: v + z_in[i, t].astype(F32), z_out[t, z].astype(F32)
        )
    await_bytes(cc, endsem.at[1])
    gv_out[...] = lax.fori_loop(
        0, PLANE - 1, lambda i, v: v + cc[i].astype(F32), rc[y, x].astype(F32)
    )
    sends.finish()


def shards(features, queries, cotangent, key_weight, value_weight):
    def vm(*shape, dtype=BF16):
        return pltpu.VMEM(shape, dtype)

    sem = pltpu.SemaphoreType.DMA
    t = 2 * NQ
    scratch = [
        vm(D, HALF), vm(D, HALF), vm(128, D), vm(2, 128, 2 * HALF),
        vm(ALL, D), vm(OWN, 2 * HALF), vm(8, 4, 4, 16, ALL),
        vm(ALL, HALF), vm(ALL, HALF), vm(ALL, 2 * HALF, dtype=F32), vm(ALL, 2 * HALF),
        vm(OWN, 2 * HALF), vm(ALL, D), vm(2, 128, 2 * HALF), vm(128, D),
        vm(192, D), vm(64, D),
        vm(NQ, 4, 8, 4, 16, 128), vm(NQ, 4, 8, 4, 16, 128), vm(8, 4, 4, 16, HALF),
        vm(t, 4, 4, 16, 128), vm(t, 4, 4, 16, 128), vm(t, 8, 4, 16, 128), vm(t, 8, 4, 16, 128),
        vm(t, 8, 4, 16, 128),
        vm(t, 4, 16, 128), vm(t, 4, 16, 128), vm(t, 8, 16, 128), vm(t, 8, 16, 128),
        vm(t, 8, 16, 128), vm(NZ - 1, t, 16, 128),
        vm(14, 2, 4, 16, HALF), vm(4, 4, 16, HALF), vm(PLANE - 1, 16, HALF),
        sem((160,)), sem((2,)), sem((4,)), sem((16,)), sem((8,)), sem((6,)),
        sem((t, 6)), sem((t, 6)), sem((14,)), sem((2,)),
    ]
    vmem = pl.BlockSpec(memory_space=pltpu.VMEM)
    hbm = pl.BlockSpec(memory_space=pl.ANY)
    return pl.pallas_call(
        kernel,
        out_shape=(
            jax.ShapeDtypeStruct(queries.shape, BF16),
            jax.ShapeDtypeStruct(features.shape, BF16),
            jax.ShapeDtypeStruct(queries.shape, BF16),
            jax.ShapeDtypeStruct((16, HALF), F32),
            jax.ShapeDtypeStruct((16, HALF), F32),
        ),
        in_specs=[vmem, vmem, vmem, hbm, hbm],
        out_specs=[vmem] * 5,
        scratch_shapes=scratch,
        compiler_params=pltpu.CompilerParams(
            collective_id=0, has_side_effects=True, vmem_limit_bytes=52 * MIB
        ),
    )(features, queries, cotangent, key_weight, value_weight)


def solution(mesh):
    rows = P("tm", "space", None)
    return jax.shard_map(
        shards,
        mesh=mesh,
        in_specs=(rows, rows, rows, P(None, "space"), P(None, "space")),
        out_specs=(rows, rows, rows, P("tm", "space"), P("tm", "space")),
        check_vma=False,
    )
```

time: 1410 us -> 79.5 us (0.06)
  the two profiles are of different devices: /device:TPU:0 before, /device:TPU:32 now
where the time goes in v2:
time: 79.5 us; the launch traced here: 79 us
  Pallas kernels  73 us (92%)
  local copies, waits for them, and re-layouts  5.32 us (7%)
    pallas_call x1, Pallas kernels, shards(): pl.pallas_call(kernel, out_shape=(jax.ShapeDtypeStruct(queries.shape, BF1...  73 us
    unnamed x9, local copies, waits for them, and re-layouts  5.32 us

profile of v2, /device:TPU:32, one launch (start us, length us, event | category | flops | bytes accessed | tf_op | source)
XLA Modules:
  0.0 79.0 jit_solution(7674964935261459758)
XLA Ops:
  0.6 0.0 copy-start
  0.6 0.9 %copy-done = bf16[2,64,1024]{2,1,0:T(8,128)(2,1)S(1)} copy-done((bf16[2,64,1024]{2,1,0:T(8,128)(2,1)S(1)}, bf16[2,64,1024]{2,1,0:T(8,128)(2,1)}, u32[]{:S(2)}) %copy-start) | copy-done | bytes 262168
  1.6 0.0 copy-start.1
  1.6 0.9 %copy-done.1 = bf16[2,64,1024]{2,1,0:T(8,128)(2,1)S(1)} copy-done((bf16[2,64,1024]{2,1,0:T(8,128)(2,1)S(1)}, bf16[2,64,1024]{2,1,0:T(8,128)(2,1)}, u32[]{:S(2)}) %copy-start.1) | copy-done | bytes 262168
  2.5 73.0 %shard_map.92 = (bf16[2,64,1024]{2,1,0:T(8,128)(2,1)S(1)}, bf16[2,64,2048]{2,1,0:T(8,128)(2,1)S(1)}, bf16[2,64,1024]{2,1,0:T(8,128)(2,1)S(1)}, f32[16,512]{1,0:T(8,128)S(1)}, f32[16,512]{1,0:T(8,128)S(1)}) custom-call(bf16[2,64,2048]{2,1,0:T(8,128)(2,1)} %f_ref.1, bf16[2,64,1024]{2,1,0:T(8,128)(2,1)S(1)} %copy-done, bf16[2,64,1024]{2,1,0:T(8,128)(2,1)S(1)} %copy-done.1, ...), custom_call_target="tpu_custom_call" | custom-call | tf_op jit(solution)/shard_map/pallas_call | solution.py:472
  75.5 0.7 copy.15
  76.2 0.8 %copy.16 = bf16[2,64,2048]{2,1,0:T(8,128)(2,1)} copy(bf16[2,64,2048]{2,1,0:T(8,128)(2,1)S(1)} %get-tuple-element.11) | data formatting | bytes 1048576
  77.0 0.7 copy.17
  77.7 0.6 copy.18
  78.4 0.6 copy.19
Async XLA Ops:
  0.6 1.0 %copy-start = (bf16[2,64,1024]{2,1,0:T(8,128)(2,1)S(1)}, bf16[2,64,1024]{2,1,0:T(8,128)(2,1)}, u32[]{:S(2)}) copy-start(bf16[2,64,1024]{2,1,0:T(8,128)(2,1)} %q_ref.1) | copy-start | bytes 786436
  1.6 0.9 %copy-start.1 = (bf16[2,64,1024]{2,1,0:T(8,128)(2,1)S(1)}, bf16[2,64,1024]{2,1,0:T(8,128)(2,1)}, u32[]{:S(2)}) copy-start(bf16[2,64,1024]{2,1,0:T(8,128)(2,1)} %c_ref.1) | copy-start | bytes 786436

commit v3 on v2

v3 whole, which is shorter than its diff:
```python
import jax
import jax.numpy as jnp
from jax import lax
from jax.experimental import pallas as pl
from jax.experimental.pallas import tpu as pltpu
from jax.sharding import PartitionSpec as P

HEAD = 128
WINDOW = 16
PLANE = 16
NZ = 8
OWN = 256
HALO = 128
ALL = HALO + OWN
HALF = 512
D = 2048
F32 = jnp.float32
BF16 = jnp.bfloat16
MIB = 2**20


def mm(a, b, ca, cb):
    return lax.dot_general(a, b, (((ca,), (cb,)), ((), ())), preferred_element_type=F32)


def rows_at(ref, start, count):
    return ref.at[pl.ds(pl.multiple_of(start, 16), count)]


def signal(sem, tm, core):
    pl.semaphore_signal(
        sem, inc=1, device_id=(tm, core), device_id_type=pl.DeviceIdType.MESH
    )


def await_bytes(ref, sem):
    pltpu.make_async_copy(ref, ref, sem).wait()


class Sends:
    def __init__(self, sems):
        self.sems, self.used, self.waits = sems, 0, []

    def start(self, src, dst, rsem, tm, core, self_if=None):
        copy = pltpu.make_async_remote_copy(
            src_ref=src, dst_ref=dst, send_sem=self.sems.at[self.used], recv_sem=rsem,
            device_id=(tm, core), device_id_type=pl.DeviceIdType.MESH,
        )
        self.used += 1
        if self_if is None:
            copy.start()
        else:
            pl.when(self_if)(lambda: pltpu.make_async_copy(src, dst, rsem).start())
            pl.when(jnp.logical_not(self_if))(copy.start)
        self.waits.append((copy, self_if))

    def settle(self, i):
        if self.waits[i] is None:
            return
        copy, self_if = self.waits[i]
        self.waits[i] = None
        if self_if is None:
            copy.wait_send()
        else:
            pl.when(jnp.logical_not(self_if))(copy.wait_send)

    def finish(self):
        for i in range(self.used):
            self.settle(i)


class Ring4:
    def __init__(self, sends, view, up, down, bufs, sems, out):
        self.sends, self.view, self.up, self.down = sends, view, up, down
        self.bufs, self.sems, self.out = bufs, sems, out

    def first(self):
        self.sends.start(self.view(2, 0), self.bufs[0], self.sems.at[0], *self.up)
        self.sends.start(self.view(2, 1), self.bufs[1], self.sems.at[1], *self.down)

    def direct(self):
        _, _, below, above = self.bufs
        h = below.shape[0] // 2
        self.sends.start(self.view(1, 1), below.at[pl.ds(h, h)], self.sems.at[2], *self.up)
        self.sends.start(self.view(3, 0), above.at[pl.ds(0, h)], self.sems.at[3], *self.down)

    def second(self):
        from_below, from_above, below, above = self.bufs
        h = below.shape[0] // 2
        for buf, sem, view, dst, dsem, dev in (
            (from_below, 0, self.view(1, 0), below.at[pl.ds(0, h)], 4, self.up),
            (from_above, 1, self.view(3, 1), above.at[pl.ds(h, h)], 5, self.down),
        ):
            await_bytes(buf, self.sems.at[sem])

            def add(i, _):
                buf[i] = (buf[i].astype(F32) + view[i].astype(F32)).astype(BF16)
                return 0

            lax.fori_loop(0, h, add, 0)
            self.sends.start(buf, dst, self.sems.at[dsem], *dev)

    def third(self):
        _, _, below, above = self.bufs
        h = below.shape[0] // 2
        await_bytes(below.at[pl.ds(h, h)], self.sems.at[2])
        await_bytes(above.at[pl.ds(0, h)], self.sems.at[3])
        await_bytes(below.at[pl.ds(0, h)], self.sems.at[4])
        await_bytes(above.at[pl.ds(h, h)], self.sems.at[5])
        for half in range(2):
            own = self.view(0, half)

            def add(i, _):
                j = half * h + i
                self.out[j] = (
                    own[i].astype(F32) + below[j].astype(F32) + above[j].astype(F32)
                ).astype(BF16)
                return 0

            lax.fori_loop(0, h, add, 0)


NA, NB = 2, 2
NT = NA + NB
CW = 1024 - 128 * NT
ORDER = (
    "p01", "p00", "T0", "B0", "a0", "p10", "gfH", "p11", "F", "gf0", "T1", "gf", "c26", "B1",
    "S0", "S2", "S1", "S3", "a1", "c170", "T2", "H0", "H2", "H1", "H3", "home1", "home2", "B2",
    "L0", "L2", "L1", "L3", "T3", "att", "M0", "M2", "M1", "M3", "Z", "gfout", "C",
)
CHAINS = ((1, 0, 4, 0), (-1, 1, 4, 4), (1, 1, 3, 8), (-1, 0, 3, 11))


def kernel(
    f_hbm, q_hbm, c_hbm, kw_hbm, vw_hbm,
    att_out, gf_out, gq_out, gk_out, gv_out,
    f_ref, q_ref, c_ref, kw, vw, fb, qcb, rows, qc, rt, k_scr, v_scr, acc, g, ag, gfp, rag, rgf, gx, gh,
    wa, wb, wc, ring_up, ring_down, ring_below, ring_above, plane_out,
    ring2_up, ring2_down, ring2_below, ring2_above, z_out, z_in, cb, rc, cc,
    send, wsem, got, qsem, fsem, hsem, gsem, r1sem, r2sem, csem, endsem,
):
    tm = lax.axis_index("tm")
    s = lax.axis_index("space")
    z, c = tm // PLANE, tm % PLANE
    y, x = c // 4, c % 4
    base = z * PLANE
    zi = [(z + r) % NZ for r in range(NZ)]
    yi = [(y + r) % 4 for r in range(4)]
    xi = [(x + r) % 4 for r in range(4)]
    nxt, prv = zi[1] * PLANE + c, zi[7] * PLANE + c

    loads = [
        pltpu.make_async_copy(src, dst, wsem.at[i])
        for i, (src, dst) in enumerate(
            ((f_hbm, f_ref), (q_hbm, q_ref), (c_hbm, c_ref), (kw_hbm, kw), (vw_hbm, vw))
        )
    ]
    loads[0].start()
    barrier = pltpu.get_barrier_semaphore()
    for r in range(1, PLANE):
        for core in range(2):
            signal(barrier, base + (c + r) % PLANE, core)
    signal(barrier, base + c, 1 - s)
    for r in range(1, NZ):
        signal(barrier, zi[r] * PLANE + c, s)

    def pack(ref, out, cols, at):
        w = cols[1] - cols[0]
        for t in range(4):
            p, q = (ref[i, 16 * t : 16 * t + 16, cols[0] : cols[1]].astype(F32) for i in range(2))
            out[32 * t : 32 * t + 32, at : at + w] = jnp.concatenate(
                [p[:8], q[:8], p[8:], q[8:]], axis=0
            ).astype(BF16)

    for copy in loads[1:]:
        copy.start()
    loads[0].wait()
    pack(f_ref, fb, (0, D), 0)
    pl.semaphore_wait(barrier, 2 * (PLANE - 1) + 1 + NZ - 1)

    sends = Sends(send)
    home = c % 2
    slot = 16 * (c // 2)
    to = (c // 4) % 2
    mine = c % 2 == s
    for r in range(8):
        j = (c // 2 + r) % 8
        sends.start(
            rows_at(fb, 16 * j, 16), rows_at(rows, HALO + 16 * c, 16), fsem.at[c],
            base + 2 * j + s, to, (mine & (to == s)) if r == 0 else None,
        )
    loads[1].wait()
    loads[2].wait()
    for pair in range(2):
        for core in range(2):
            at = HALF * core + 256 * pair
            pack(q_ref, qcb.at[core, pair], (at, at + 256), 0)
            pack(c_ref, qcb.at[core, pair], (at, at + 256), 256)
    for pair in range(2):
        for r in range(8):
            j = (c // 2 + r) % 8
            if pair == 0:
                sends.settle(r)
            for o in range(2):
                core = (s + o) % 2
                sends.start(
                    rows_at(qcb.at[core, pair], 16 * j, 16), rows_at(qc.at[pair], 16 * c, 16),
                    qsem.at[pair], base + 2 * j + s, core, mine if r == 0 and o == 0 else None,
                )
    for r in range(4):
        i = 4 * s + xi[r]
        block = rows_at(rows, HALO + 128 + 16 * i, 16)
        await_bytes(block, fsem.at[8 + i])
        sends.start(block, rows_at(rows, 16 * i, 16), hsem.at[i], nxt, s)
        sends.start(block, block, got.at[0], base + c, 1 - s)
    for r in range(4):
        i = 4 * s + xi[r]
        block = rows_at(rows, HALO + 16 * i, 16)
        await_bytes(block, fsem.at[i])
        sends.start(block, block, got.at[1], base + c, 1 - s)

    def project(lo):
        part = rows[lo : lo + 128, :]
        k_scr[lo : lo + 128, :] = mm(part, kw[...], 1, 0).astype(BF16)
        v_scr[lo : lo + 128, :] = mm(part, vw[...], 1, 0).astype(BF16)
        rt[:, :, :, :, lo : lo + 128] = part.T.reshape(8, 4, 4, 16, 128)

    def other(lo):
        return rows_at(rows, lo + 64 * (1 - s), 64)

    loads[3].wait()
    loads[4].wait()
    await_bytes(other(HALO + 128), got.at[0])
    project(HALO + 128)
    await_bytes(other(HALO), got.at[1])
    project(HALO)
    acc[...] = jnp.zeros_like(acc)

    def gf_make(lo, count):
        gfp[lo : lo + count, :] = (
            mm(g[lo : lo + count, 0:256], kw[:, 0:256], 1, 1)
            + mm(g[lo : lo + count, 256:512], vw[:, 0:256], 1, 1)
            + mm(g[lo : lo + count, 512:768], kw[:, 256:512], 1, 1)
            + mm(g[lo : lo + count, 768:1024], vw[:, 256:512], 1, 1)
        ).astype(BF16)

    def gf_cross(i):
        sends.start(
            rows_at(gfp, 128 * i + 64 * (1 - s), 64), gx.at[pl.ds(64 * i, 64)],
            gsem.at[1 + i], base + c, 1 - s,
        )

    def gf_add(i):
        await_bytes(gx.at[pl.ds(64 * i, 64)], gsem.at[1 + i])

        def add(t, _):
            there = pl.ds(pl.multiple_of(64 * i + 16 * t, 16), 16)
            here = pl.ds(pl.multiple_of(128 * i + 64 * s + 16 * t, 16), 16)
            gx[there] = (gx[there].astype(F32) + gfp[here].astype(F32)).astype(BF16)
            return 0

        lax.fori_loop(0, 4, add, 0)

    def gf_home(i):
        for r in range(4):
            t = (c + r) % 4
            d = 8 * (i - 1) + 4 * s + t
            sends.start(
                rows_at(gx, 64 * i + 16 * t, 16), rows_at(rgf, slot, 16), gsem.at[5],
                base + d, home, ((d == c) & (home == s)) if r == 0 else None,
            )

    scale = HEAD ** -0.5
    n = OWN // 2
    col = lax.broadcasted_iota(jnp.int32, (n, 2 * n), 1)
    back = lax.broadcasted_iota(jnp.int32, (n, 2 * n), 0) + HALO - col
    window = (back >= 0) & (back < 8 * WINDOW) & (back % 8 == 0)
    keep = (window & ((z > 0) | (col >= HALO)), window)

    def attend(pair, tile):
        lo = tile * n
        for h in range(2):
            cols = slice(128 * h, 128 * h + 128)
            vcols = slice(256 + 128 * h, 384 + 128 * h)
            at = 512 * pair + 128 * h
            head = slice(256 * pair + 128 * h, 256 * pair + 128 * h + 128)
            q = qc[pair, lo : lo + n, cols]
            cot = qc[pair, lo : lo + n, vcols]
            k = k_scr[lo : lo + 2 * n, head]
            v = v_scr[lo : lo + 2 * n, head]
            scores = jnp.where(keep[tile], mm(q, k, 1, 1) * scale, -jnp.inf)
            e = jnp.exp(scores - jnp.max(scores, axis=-1, keepdims=True))
            w = e / jnp.sum(e, axis=-1, keepdims=True)
            rounded = w.astype(BF16)
            dp = mm(cot, v, 1, 1)
            spread = jnp.sum(w * dp, axis=-1, keepdims=True)
            ds = (w * (dp - spread) * scale).astype(BF16)
            ag[pair, lo : lo + n, cols] = mm(rounded, v, 1, 0).astype(BF16)
            ag[pair, lo : lo + n, vcols] = mm(ds, k, 1, 0).astype(BF16)
            acc[lo : lo + 2 * n, at : at + 128] += mm(ds, q, 0, 0)
            acc[lo : lo + 2 * n, at + 256 : at + 384] += mm(rounded, cot, 0, 0)

    def ag_home(pair, tile):
        for r in range(8):
            d = 8 * tile + (c + r) % 8
            sends.start(
                rows_at(ag.at[pair], 16 * d, 16), rows_at(rag.at[s, pair], slot, 16), gsem.at[0],
                base + d, home, ((home == s) & (d == c)) if r == 0 else None,
            )

    def c_view(r, h):
        return wc.at[r % NZ, pl.ds(2 * h, 2)]

    def c_make(*steps):
        for r in steps:
            wc[r] = mm(rt[zi[r]].reshape(256, ALL), g[:, :CW], 1, 0).astype(BF16).reshape(
                4, 4, 16, CW
            )

    def c_step(chains, k):
        for way, h, length, first in chains:
            own = c_view(way * (length - k), h)
            src = own
            if k > 0:
                src = cb.at[first + k - 1]
                await_bytes(src, csem.at[first + k - 1])

                def add(i, _):
                    src[i] = (src[i].astype(F32) + own[i].astype(F32)).astype(BF16)
                    return 0

                lax.fori_loop(0, 2, add, 0)
            sends.start(src, cb.at[first + k], csem.at[first + k], nxt if way == 1 else prv, s)

    def ab_make(out, r, lhs, lo, count):
        v = mm(lhs.reshape(512, ALL), g[:, lo : lo + 128 * count], 1, 0).astype(BF16)
        for t in range(count):
            out[t, r] = v[:, 128 * t : 128 * t + 128].reshape(8, 4, 16, 128)

    up_x, down_x = (base + y * 4 + xi[1], s), (base + y * 4 + xi[3], s)
    up_y, down_y = (base + yi[1] * 4 + x, s), (base + yi[3] * 4 + x, s)
    plane_rings, line_rings = [], []
    for t in range(NT):
        part, q = (0, t) if t < NA else (1, t - NA)
        own = (wa, wb)[part].at[q]
        mid = plane_out.at[t]
        over = (yi, xi)[part]
        plane_rings.append(Ring4(
            sends, lambda r, h, own=own: own.at[r, pl.ds(4 * h, 4)],
            *((up_x, down_x), (up_y, down_y))[part],
            (ring_up.at[t], ring_down.at[t], ring_below.at[t], ring_above.at[t]),
            r1sem.at[t], mid,
        ))
        line_rings.append(Ring4(
            sends, lambda r, h, mid=mid, over=over: mid.at[pl.ds(4 * h, 4), over[r]],
            *((up_y, down_y), (up_x, down_x))[part],
            (ring2_up.at[t], ring2_down.at[t], ring2_below.at[t], ring2_above.at[t]),
            r2sem.at[t], z_out.at[t],
        ))

    def a_make(r):
        ab_make(wa, r, rt[:, :, xi[r]], CW, NA)

    def b_make(r):
        ab_make(wb, r, rt[:, yi[r]], CW + 128 * NA, NB)

    def ring_start():
        a_make(2)
        for t in range(NA):
            plane_rings[t].first()
        b_make(2)
        for t in range(NA, NT):
            plane_rings[t].first()
        a_make(1)
        a_make(3)
        for t in range(NA):
            plane_rings[t].direct()
        b_make(1)
        b_make(3)
        for t in range(NA, NT):
            plane_rings[t].direct()

    def c_first():
        c_make(4)
        c_step(CHAINS[:2], 0)

    def c_second():
        c_make(3, 5)
        c_step(CHAINS[2:], 0)

    def gf_own():
        gf_make(HALO, OWN)
        gf_cross(1)
        gf_cross(2)

    def gf_home1():
        gf_add(1)
        gf_home(1)

    def gf_home2():
        gf_add(2)
        await_bytes(gh, gsem.at[4])

        def add_halo(t, _):
            there = pl.ds(pl.multiple_of(128 + 16 * t, 16), 16)
            here = pl.ds(pl.multiple_of(16 * t, 16), 16)
            gx[there] = (gx[there].astype(F32) + gh[here].astype(F32)).astype(BF16)
            return 0

        lax.fori_loop(0, 4, add_halo, 0)
        gf_home(2)

    def own_slices():
        c_make(1, 7, 0)
        a_make(0)
        b_make(0)

    def to_line(t):
        plane_rings[t].third()
        line_rings[t].first()
        line_rings[t].direct()

    def unpack(value):
        v = value.astype(F32)
        return (
            jnp.concatenate([v[0:8], v[16:24]], axis=0).astype(BF16),
            jnp.concatenate([v[8:16], v[24:32]], axis=0).astype(BF16),
        )

    def att_unpack():
        await_bytes(rag, gsem.at[0])
        for core in range(2):
            for pair in range(2):
                to = HALF * core + 256 * pair
                for out, at in ((att_out, 0), (gq_out, 256)):
                    for t in range(4):
                        part = rag[core, pair, 32 * t : 32 * t + 32, at : at + 256]
                        for fr, v in enumerate(unpack(part)):
                            out[fr, 16 * t : 16 * t + 16, to : to + 256] = v

    def gf_unpack():
        await_bytes(rgf, gsem.at[5])
        for t in range(4):
            for fr, v in enumerate(unpack(rgf[32 * t : 32 * t + 32, :])):
                gf_out[fr, 16 * t : 16 * t + 16, :] = v

    def z_sends():
        for r in range(1, NZ):
            sends.start(z_out.at[:, zi[r]], z_in.at[r - 1], endsem.at[0], zi[r] * PLANE + c, s)

    def c_last():
        for way, h, length, first in CHAINS:
            await_bytes(cb.at[first + length - 1], csem.at[first + length - 1])
        for h, (p, m) in enumerate(((3, 13), (10, 7))):
            own = c_view(0, h)

            def add(i, _):
                rc[2 * h + i] = (
                    own[i].astype(F32) + cb[p, i].astype(F32) + cb[m, i].astype(F32)
                ).astype(BF16)
                return 0

            lax.fori_loop(0, 2, add, 0)
        for r in range(1, PLANE):
            yy, xx = yi[r // 4], xi[r % 4]
            sends.start(rc.at[yy, xx], cc.at[r - 1], endsem.at[1], base + yy * 4 + xx, s)

    def halo_relay():
        for r in range(4):
            i = 4 * s + xi[r]
            block = rows_at(rows, 16 * i, 16)
            await_bytes(block, hsem.at[i])
            sends.start(block, block, got.at[2], base + c, 1 - s)

    def first_heads(tile):
        if tile == 1:
            await_bytes(qc.at[0], qsem.at[0])
        else:
            halo_relay()
            await_bytes(other(0), got.at[2])
            project(0)
        attend(0, tile)
        if tile == 0:
            g[:, :512] = acc[:, :512].astype(BF16)

    def second_heads(tile):
        if tile == 0:
            await_bytes(qc.at[1], qsem.at[1])
        attend(1, tile)
        if tile == 1:
            g[HALO:, 512:] = acc[HALO:, 512:].astype(BF16)

    def gf_halo():
        g[:HALO, 512:] = acc[:HALO, 512:].astype(BF16)
        gf_make(0, HALO)
        gf_cross(0)

    def gf_back():
        gf_add(0)
        sends.start(gx.at[pl.ds(0, 64)], gh, gsem.at[4], prv, s)

    steps = {
        "p01": lambda: first_heads(1), "p00": lambda: first_heads(0),
        "p10": lambda: second_heads(0), "p11": lambda: second_heads(1),
        "a0": lambda: (ag_home(0, 1), ag_home(0, 0)), "a1": lambda: (ag_home(1, 0), ag_home(1, 1)),
        "gfH": gf_halo, "gf0": gf_back,
        "T0": c_first, "B0": c_second, "F": ring_start, "gf": gf_own, "home1": gf_home1,
        "home2": gf_home2, "c26": lambda: c_make(2, 6), "c170": own_slices,
        "att": att_unpack, "gfout": gf_unpack, "Z": z_sends, "C": c_last,
    }
    for k in range(1, 4):
        steps["T%d" % k] = lambda k=k: c_step(CHAINS[:2], k)
        steps["B%d" % k] = lambda k=k: c_step(CHAINS[2:], k)
    for t in range(NT):
        steps["S%d" % t] = plane_rings[t].second
        steps["H%d" % t] = lambda t=t: to_line(t)
        steps["L%d" % t] = line_rings[t].second
        steps["M%d" % t] = line_rings[t].third
    for name in ORDER:
        steps[name]()

    await_bytes(z_in, endsem.at[0])
    for t in range(NT):
        out, at = (gk_out, 256 + 128 * t) if t < NA else (gv_out, 256 + 128 * (t - NA))
        out[:, at : at + 128] = lax.fori_loop(
            0, NZ - 1, lambda i, v: v + z_in[i, t].astype(F32), z_out[t, z].astype(F32)
        )
    await_bytes(cc, endsem.at[1])
    last = lax.fori_loop(
        0, PLANE - 1, lambda i, v: v + cc[i].astype(F32), rc[y, x].astype(F32)
    )
    gk_out[:, 0:256] = last[:, 0:256]
    gv_out[:, 0:256] = last[:, 256:512]
    sends.finish()


def leave_kernel(*refs):
    into, out = (
        [pltpu.make_async_copy(src[i], dst[i], sem.at[i]) for i in range(5)]
        for src, dst, sem in ((refs[0:5], refs[10:15], refs[15]), (refs[10:15], refs[5:10], refs[16]))
    )
    for copy in into:
        copy.start()
    for i in range(5):
        into[i].wait()
        out[i].start()
    for copy in out:
        copy.wait()


def shards(features, queries, cotangent, key_weight, value_weight):
    def vm(*shape, dtype=BF16):
        return pltpu.VMEM(shape, dtype)

    sem = pltpu.SemaphoreType.DMA
    t = NT
    scratch = [
        vm(2, 64, D), vm(2, 64, 2 * HALF), vm(2, 64, 2 * HALF),
        vm(D, HALF), vm(D, HALF), vm(128, D), vm(2, 2, 128, HALF),
        vm(ALL, D), vm(2, OWN, HALF), vm(8, 4, 4, 16, ALL),
        vm(ALL, HALF), vm(ALL, HALF), vm(ALL, 2 * HALF, dtype=F32), vm(ALL, 2 * HALF),
        vm(2, OWN, HALF), vm(ALL, D), vm(2, 2, 128, HALF), vm(128, D),
        vm(192, D), vm(64, D),
        vm(NA, 4, 8, 4, 16, 128), vm(NB, 4, 8, 4, 16, 128), vm(8, 4, 4, 16, CW),
        vm(t, 4, 4, 16, 128), vm(t, 4, 4, 16, 128), vm(t, 8, 4, 16, 128), vm(t, 8, 4, 16, 128),
        vm(t, 8, 4, 16, 128),
        vm(t, 4, 16, 128), vm(t, 4, 16, 128), vm(t, 8, 16, 128), vm(t, 8, 16, 128),
        vm(t, 8, 16, 128), vm(NZ - 1, t, 16, 128),
        vm(14, 2, 4, 16, CW), vm(4, 4, 16, CW), vm(PLANE - 1, 16, CW),
        sem((200,)), sem((5,)), sem((3,)), sem((2,)), sem((16,)), sem((8,)), sem((6,)),
        sem((t, 6)), sem((t, 6)), sem((14,)), sem((2,)),
    ]
    vmem = pl.BlockSpec(memory_space=pltpu.VMEM)
    hbm = pl.BlockSpec(memory_space=pl.ANY)
    results = pl.pallas_call(
        kernel,
        out_shape=(
            jax.ShapeDtypeStruct(queries.shape, BF16),
            jax.ShapeDtypeStruct(features.shape, BF16),
            jax.ShapeDtypeStruct(queries.shape, BF16),
            jax.ShapeDtypeStruct((16, HALF), F32),
            jax.ShapeDtypeStruct((16, HALF), F32),
        ),
        in_specs=[hbm] * 5,
        out_specs=[vmem] * 5,
        scratch_shapes=scratch,
        compiler_params=pltpu.CompilerParams(
            collective_id=0, has_side_effects=True, vmem_limit_bytes=61 * MIB
        ),
    )(features, queries, cotangent, key_weight, value_weight)
    return pl.pallas_call(
        leave_kernel,
        out_shape=tuple(jax.ShapeDtypeStruct(v.shape, v.dtype) for v in results),
        in_specs=[hbm] * 5,
        out_specs=[hbm] * 5,
        scratch_shapes=[pltpu.VMEM(v.shape, v.dtype) for v in results] + [sem((5,)), sem((5,))],
        compiler_params=pltpu.CompilerParams(vmem_limit_bytes=61 * MIB),
    )(*results)


def solution(mesh):
    rows = P("tm", "space", None)
    return jax.shard_map(
        shards,
        mesh=mesh,
        in_specs=(rows, rows, rows, P(None, "space"), P(None, "space")),
        out_specs=(rows, rows, rows, P("tm", "space"), P("tm", "space")),
        check_vma=False,
    )
```

time: 79.5 us -> 71.1 us (0.89)
  local copies, waits for them, and re-layouts: 5.32 us -> 0 us
  Pallas kernels: 73 us -> 69.3 us
    pallas_call x1, Pallas kernels: 73 us -> 67.2 us  [shards(): pl.pallas_call(kernel, out_shape=(jax.ShapeDtypeStruct(queries.shape, BF1...]
    unnamed x9 -> x0, local copies, waits for them, and re-layouts: 5.32 us -> none
    pallas_call x0 -> x1, Pallas kernels: none -> 2.1 us  [shards(): pl.pallas_call(leave_kernel, out_shape=tuple((jax.ShapeDtypeStruct(v.shap...]
where the time goes in v3:
time: 71.1 us; the launch traced here: 70 us
  Pallas kernels  69.3 us (97%)
    pallas_call x1, Pallas kernels, shards(): pl.pallas_call(kernel, out_shape=(jax.ShapeDtypeStruct(queries.shape, BF1...  67.2 us
    pallas_call x1, Pallas kernels, shards(): pl.pallas_call(leave_kernel, out_shape=tuple((jax.ShapeDtypeStruct(v.shap...  2.1 us

profile of v3, /device:TPU:32, one launch (start us, length us, event | category | flops | bytes accessed | tf_op | source)
XLA Modules:
  0.0 70.0 jit_solution(2701793619486078310)
XLA Ops:
  0.6 67.2 %shard_map.92 = (bf16[2,64,1024]{2,1,0:T(8,128)(2,1)}, bf16[2,64,2048]{2,1,0:T(8,128)(2,1)}, bf16[2,64,1024]{2,1,0:T(8,128)(2,1)}, f32[16,512]{1,0:T(8,128)}, f32[16,512]{1,0:T(8,128)}) custom-call(bf16[2,64,2048]{2,1,0:T(8,128)(2,1)} %f_hbm.1, bf16[2,64,1024]{2,1,0:T(8,128)(2,1)} %q_hbm.1, bf16[2,64,1024]{2,1,0:T(8,128)(2,1)} %c_hbm.1, ...), custom_call_target="tpu_custom_call" | custom-call | tf_op jit(solution)/shard_map/pallas_call | solution.py:575
  67.9 2.1 %shard_map.93 = (bf16[2,64,1024]{2,1,0:T(8,128)(2,1)}, bf16[2,64,2048]{2,1,0:T(8,128)(2,1)}, bf16[2,64,1024]{2,1,0:T(8,128)(2,1)}, f32[16,512]{1,0:T(8,128)}, f32[16,512]{1,0:T(8,128)}) custom-call(bf16[2,64,1024]{2,1,0:T(8,128)(2,1)} %get-tuple-element.10.refs_0_, bf16[2,64,2048]{2,1,0:T(8,128)(2,1)} %get-tuple-element.11.refs_1_, ...), custom_call_target="tpu_custom_call" | custom-call | tf_op jit(solution)/shard_map/pallas_call | solution.py:591

commit v4 on v3

--- a/solution.py
+++ b/solution.py
@@ -124,20 +124,43 @@
 NT = NA + NB
 CW = 1024 - 128 * NT
 ORDER = (
-    "p01", "p00", "T0", "B0", "a0", "p10", "gfH", "p11", "F", "gf0", "T1", "gf", "c26", "B1",
-    "S0", "S2", "S1", "S3", "a1", "c170", "T2", "H0", "H2", "H1", "H3", "home1", "home2", "B2",
-    "L0", "L2", "L1", "L3", "T3", "att", "M0", "M2", "M1", "M3", "Z", "gfout", "C",
+    "p01", "a01", "p00", "T0", "B0", "a00", "p10", "gfH", "p11", "F", "gf0", "T1", "gf", "c26",
+    "B1", "S0", "S2", "S1", "S3", "c170", "T2", "H0", "H2", "H1", "H3", "a10", "a11", "home1",
+    "home2", "B2", "T3", "M0", "M2", "M1", "M3", "Z", "C", "att", "gfout",
 )
+class Line4:
+    def __init__(self, sends, mine, slices, devices, buf, sem, out):
+        self.sends, self.mine, self.slices, self.devices = sends, mine, slices, devices
+        self.buf, self.sem, self.out = buf, sem, out
+
+    def start(self):
+        for r, (piece, device) in enumerate(zip(self.slices, self.devices)):
+            self.sends.start(piece, self.buf.at[r], self.sem, *device)
+
+    def finish(self):
+        await_bytes(self.buf, self.sem)
+
+        def add(i, _):
+            total = self.mine[i].astype(F32)
+            for r in range(3):
+                total += self.buf[r, i].astype(F32)
+            self.out[i] = total.astype(BF16)
+            return 0
+
+        lax.fori_loop(0, NZ, add, 0)
+
+
 CHAINS = ((1, 0, 4, 0), (-1, 1, 4, 4), (1, 1, 3, 8), (-1, 0, 3, 11))
 
 
 def kernel(
     f_hbm, q_hbm, c_hbm, kw_hbm, vw_hbm,
+    att_hbm, gf_hbm, gq_hbm, gk_hbm, gv_hbm,
     att_out, gf_out, gq_out, gk_out, gv_out,
     f_ref, q_ref, c_ref, kw, vw, fb, qcb, rows, qc, rt, k_scr, v_scr, acc, g, ag, gfp, rag, rgf, gx, gh,
     wa, wb, wc, ring_up, ring_down, ring_below, ring_above, plane_out,
-    ring2_up, ring2_down, ring2_below, ring2_above, z_out, z_in, cb, rc, cc,
-    send, wsem, got, qsem, fsem, hsem, gsem, r1sem, r2sem, csem, endsem,
+    ring2, z_out, z_in, cb, rc, cc,
+    send, wsem, got, qsem, fsem, hsem, gsem, r1sem, r2sem, csem, endsem, osem,
 ):
     tm = lax.axis_index("tm")
     s = lax.axis_index("space")
@@ -152,10 +175,17 @@
     loads = [
         pltpu.make_async_copy(src, dst, wsem.at[i])
         for i, (src, dst) in enumerate(
-            ((f_hbm, f_ref), (q_hbm, q_ref), (c_hbm, c_ref), (kw_hbm, kw), (vw_hbm, vw))
+            ((q_hbm, q_ref), (c_hbm, c_ref), (kw_hbm, kw), (vw_hbm, vw))
         )
     ]
-    loads[0].start()
+    f_loads = [
+        pltpu.make_async_copy(
+            f_hbm.at[:, 16 * t : 16 * t + 16], f_ref.at[:, 16 * t : 16 * t + 16], wsem.at[5 + t]
+        )
+        for t in range(4)
+    ]
+    for copy in f_loads:
+        copy.start()
     barrier = pltpu.get_barrier_semaphore()
     for r in range(1, PLANE):
         for core in range(2):
@@ -164,18 +194,19 @@
     for r in range(1, NZ):
         signal(barrier, zi[r] * PLANE + c, s)
 
-    def pack(ref, out, cols, at):
+    def pack(ref, out, cols, at, waits=None):
         w = cols[1] - cols[0]
         for t in range(4):
+            if waits:
+                waits[t].wait()
             p, q = (ref[i, 16 * t : 16 * t + 16, cols[0] : cols[1]].astype(F32) for i in range(2))
             out[32 * t : 32 * t + 32, at : at + w] = jnp.concatenate(
                 [p[:8], q[:8], p[8:], q[8:]], axis=0
             ).astype(BF16)
 
-    for copy in loads[1:]:
+    for copy in loads:
         copy.start()
-    loads[0].wait()
-    pack(f_ref, fb, (0, D), 0)
+    pack(f_ref, fb, (0, D), 0, f_loads)
     pl.semaphore_wait(barrier, 2 * (PLANE - 1) + 1 + NZ - 1)
 
     sends = Sends(send)
@@ -189,8 +220,8 @@
             rows_at(fb, 16 * j, 16), rows_at(rows, HALO + 16 * c, 16), fsem.at[c],
             base + 2 * j + s, to, (mine & (to == s)) if r == 0 else None,
         )
+    loads[0].wait()
     loads[1].wait()
-    loads[2].wait()
     for pair in range(2):
         for core in range(2):
             at = HALF * core + 256 * pair
@@ -228,13 +259,12 @@
     def other(lo):
         return rows_at(rows, lo + 64 * (1 - s), 64)
 
+    loads[2].wait()
     loads[3].wait()
-    loads[4].wait()
     await_bytes(other(HALO + 128), got.at[0])
     project(HALO + 128)
     await_bytes(other(HALO), got.at[1])
     project(HALO)
-    acc[...] = jnp.zeros_like(acc)
 
     def gf_make(lo, count):
         gfp[lo : lo + count, :] = (
@@ -277,28 +307,41 @@
     window = (back >= 0) & (back < 8 * WINDOW) & (back % 8 == 0)
     keep = (window & ((z > 0) | (col >= HALO)), window)
 
+    first_tile = (1, 0)
+
     def attend(pair, tile):
         lo = tile * n
-        for h in range(2):
-            cols = slice(128 * h, 128 * h + 128)
-            vcols = slice(256 + 128 * h, 384 + 128 * h)
-            at = 512 * pair + 128 * h
-            head = slice(256 * pair + 128 * h, 256 * pair + 128 * h + 128)
-            q = qc[pair, lo : lo + n, cols]
-            cot = qc[pair, lo : lo + n, vcols]
-            k = k_scr[lo : lo + 2 * n, head]
-            v = v_scr[lo : lo + 2 * n, head]
-            scores = jnp.where(keep[tile], mm(q, k, 1, 1) * scale, -jnp.inf)
-            e = jnp.exp(scores - jnp.max(scores, axis=-1, keepdims=True))
-            w = e / jnp.sum(e, axis=-1, keepdims=True)
-            rounded = w.astype(BF16)
-            dp = mm(cot, v, 1, 1)
-            spread = jnp.sum(w * dp, axis=-1, keepdims=True)
-            ds = (w * (dp - spread) * scale).astype(BF16)
-            ag[pair, lo : lo + n, cols] = mm(rounded, v, 1, 0).astype(BF16)
-            ag[pair, lo : lo + n, vcols] = mm(ds, k, 1, 0).astype(BF16)
-            acc[lo : lo + 2 * n, at : at + 128] += mm(ds, q, 0, 0)
-            acc[lo : lo + 2 * n, at + 256 : at + 384] += mm(rounded, cot, 0, 0)
+        two = range(2)
+        cols = [slice(128 * h, 128 * h + 128) for h in two]
+        vcols = [slice(256 + 128 * h, 384 + 128 * h) for h in two]
+        heads = [slice(256 * pair + 128 * h, 256 * pair + 128 * h + 128) for h in two]
+        q = [qc[pair, lo : lo + n, cols[h]] for h in two]
+        cot = [qc[pair, lo : lo + n, vcols[h]] for h in two]
+        k = [k_scr[lo : lo + 2 * n, heads[h]] for h in two]
+        v = [v_scr[lo : lo + 2 * n, heads[h]] for h in two]
+        scores = [jnp.where(keep[tile], mm(q[h], k[h], 1, 1) * scale, -jnp.inf) for h in two]
+        dp = [mm(cot[h], v[h], 1, 1) for h in two]
+        e = [jnp.exp(scores[h] - jnp.max(scores[h], axis=-1, keepdims=True)) for h in two]
+        w = [e[h] / jnp.sum(e[h], axis=-1, keepdims=True) for h in two]
+        rounded = [w[h].astype(BF16) for h in two]
+        wd = [w[h] * dp[h] for h in two]
+        spread = [jnp.sum(wd[h], axis=-1, keepdims=True) for h in two]
+        ds = [(w[h] * (dp[h] - spread[h]) * scale).astype(BF16) for h in two]
+        for h in two:
+            ag[pair, lo : lo + n, cols[h]] = mm(rounded[h], v[h], 1, 0).astype(BF16)
+            ag[pair, lo : lo + n, vcols[h]] = mm(ds[h], k[h], 1, 0).astype(BF16)
+        for at, left, right in ((0, ds, q), (256, rounded, cot)):
+            for h in two:
+                to = slice(512 * pair + at + 128 * h, 512 * pair + at + 128 * h + 128)
+                grad = mm(left[h], right[h], 0, 0)
+                if tile == first_tile[pair]:
+                    acc[lo : lo + 2 * n, to] = grad
+                elif tile == 0:
+                    acc[0:n, to] = grad[0:n]
+                    acc[n : 2 * n, to] += grad[n:]
+                else:
+                    acc[n : 2 * n, to] += grad[0:n]
+                    acc[2 * n :, to] = grad[n:]
 
     def ag_home(pair, tile):
         for r in range(8):
@@ -351,11 +394,10 @@
             (ring_up.at[t], ring_down.at[t], ring_below.at[t], ring_above.at[t]),
             r1sem.at[t], mid,
         ))
-        line_rings.append(Ring4(
-            sends, lambda r, h, mid=mid, over=over: mid.at[pl.ds(4 * h, 4), over[r]],
-            *((up_y, down_y), (up_x, down_x))[part],
-            (ring2_up.at[t], ring2_down.at[t], ring2_below.at[t], ring2_above.at[t]),
-            r2sem.at[t], z_out.at[t],
+        line_rings.append(Line4(
+            sends, mid.at[:, over[0]], [mid.at[:, over[r]] for r in range(1, 4)],
+            [((base + yi[r] * 4 + x, base + y * 4 + xi[r])[part], s) for r in range(1, 4)],
+            ring2.at[t], r2sem.at[t], z_out.at[t],
         ))
 
     def a_make(r):
@@ -417,8 +459,7 @@
 
     def to_line(t):
         plane_rings[t].third()
-        line_rings[t].first()
-        line_rings[t].direct()
+        line_rings[t].start()
 
     def unpack(value):
         v = value.astype(F32)
@@ -426,6 +467,14 @@
             jnp.concatenate([v[0:8], v[16:24]], axis=0).astype(BF16),
             jnp.concatenate([v[8:16], v[24:32]], axis=0).astype(BF16),
         )
+
+    leaving = [
+        pltpu.make_async_copy(src, dst, osem.at[i])
+        for i, (src, dst) in enumerate((
+            (att_out, att_hbm), (gq_out, gq_hbm), (gf_out, gf_hbm), (gk_out, gk_hbm),
+            (gv_out, gv_hbm),
+        ))
+    ]
 
     def att_unpack():
         await_bytes(rag, gsem.at[0])
@@ -437,12 +486,15 @@
                         part = rag[core, pair, 32 * t : 32 * t + 32, at : at + 256]
                         for fr, v in enumerate(unpack(part)):
                             out[fr, 16 * t : 16 * t + 16, to : to + 256] = v
+        leaving[0].start()
+        leaving[1].start()
 
     def gf_unpack():
         await_bytes(rgf, gsem.at[5])
         for t in range(4):
             for fr, v in enumerate(unpack(rgf[32 * t : 32 * t + 32, :])):
                 gf_out[fr, 16 * t : 16 * t + 16, :] = v
+        leaving[2].start()
 
     def z_sends():
         for r in range(1, NZ):
@@ -502,7 +554,8 @@
     steps = {
         "p01": lambda: first_heads(1), "p00": lambda: first_heads(0),
         "p10": lambda: second_heads(0), "p11": lambda: second_heads(1),
-        "a0": lambda: (ag_home(0, 1), ag_home(0, 0)), "a1": lambda: (ag_home(1, 0), ag_home(1, 1)),
+        "a01": lambda: ag_home(0, 1), "a00": lambda: ag_home(0, 0),
+        "a11": lambda: ag_home(1, 1), "a10": lambda: ag_home(1, 0),
         "gfH": gf_halo, "gf0": gf_back,
         "T0": c_first, "B0": c_second, "F": ring_start, "gf": gf_own, "home1": gf_home1,
         "home2": gf_home2, "c26": lambda: c_make(2, 6), "c170": own_slices,
@@ -514,24 +567,26 @@
     for t in range(NT):
         steps["S%d" % t] = plane_rings[t].second
         steps["H%d" % t] = lambda t=t: to_line(t)
-        steps["L%d" % t] = line_rings[t].second
-        steps["M%d" % t] = line_rings[t].third
+        steps["M%d" % t] = line_rings[t].finish
     for name in ORDER:
         steps[name]()
+
+    def gathered(buf, own, count):
+        return lax.fori_loop(0, count, lambda i, v: v + buf[i].astype(F32), own.astype(F32))
 
     await_bytes(z_in, endsem.at[0])
     for t in range(NT):
         out, at = (gk_out, 256 + 128 * t) if t < NA else (gv_out, 256 + 128 * (t - NA))
-        out[:, at : at + 128] = lax.fori_loop(
-            0, NZ - 1, lambda i, v: v + z_in[i, t].astype(F32), z_out[t, z].astype(F32)
-        )
+        out[:, at : at + 128] = gathered(z_in.at[:, t], z_out[t, z], NZ - 1)
     await_bytes(cc, endsem.at[1])
-    last = lax.fori_loop(
-        0, PLANE - 1, lambda i, v: v + cc[i].astype(F32), rc[y, x].astype(F32)
-    )
+    last = gathered(cc, rc[y, x], PLANE - 1)
     gk_out[:, 0:256] = last[:, 0:256]
     gv_out[:, 0:256] = last[:, 256:512]
+    leaving[3].start()
+    leaving[4].start()
     sends.finish()
+    for copy in leaving:
+        copy.wait()
 
 
 def leave_kernel(*refs):
@@ -555,6 +610,8 @@
     sem = pltpu.SemaphoreType.DMA
     t = NT
     scratch = [
+        vm(2, 64, 1024), vm(2, 64, D), vm(2, 64, 1024), vm(16, HALF, dtype=F32),
+        vm(16, HALF, dtype=F32),
         vm(2, 64, D), vm(2, 64, 2 * HALF), vm(2, 64, 2 * HALF),
         vm(D, HALF), vm(D, HALF), vm(128, D), vm(2, 2, 128, HALF),
         vm(ALL, D), vm(2, OWN, HALF), vm(8, 4, 4, 16, ALL),
@@ -564,11 +621,11 @@
         vm(NA, 4, 8, 4, 16, 128), vm(NB, 4, 8, 4, 16, 128), vm(8, 4, 4, 16, CW),
         vm(t, 4, 4, 16, 128), vm(t, 4, 4, 16, 128), vm(t, 8, 4, 16, 128), vm(t, 8, 4, 16, 128),
         vm(t, 8, 4, 16, 128),
-        vm(t, 4, 16, 128), vm(t, 4, 16, 128), vm(t, 8, 16, 128), vm(t, 8, 16, 128),
+        vm(t, 3, 8, 16, 128),
         vm(t, 8, 16, 128), vm(NZ - 1, t, 16, 128),
         vm(14, 2, 4, 16, CW), vm(4, 4, 16, CW), vm(PLANE - 1, 16, CW),
-        sem((200,)), sem((5,)), sem((3,)), sem((2,)), sem((16,)), sem((8,)), sem((6,)),
-        sem((t, 6)), sem((t, 6)), sem((14,)), sem((2,)),
+        sem((200,)), sem((9,)), sem((3,)), sem((2,)), sem((16,)), sem((8,)), sem((6,)),
+        sem((t, 6)), sem((t,)), sem((14,)), sem((2,)), sem((5,)),
     ]
     vmem = pl.BlockSpec(memory_space=pltpu.VMEM)
     hbm = pl.BlockSpec(memory_space=pl.ANY)
@@ -582,7 +639,7 @@
             jax.ShapeDtypeStruct((16, HALF), F32),
         ),
         in_specs=[hbm] * 5,
-        out_specs=[vmem] * 5,
+        out_specs=[hbm] * 5,
         scratch_shapes=scratch,
         compiler_params=pltpu.CompilerParams(
             collective_id=0, has_side_effects=True, vmem_limit_bytes=61 * MIB

time: 71.1 us -> 68.4 us (0.962); the launches traced: 70 us -> 68.1 us
  Pallas kernels: 69.3 us -> 67.4 us
    pallas_call x1, Pallas kernels: 67.2 us -> 65.3 us  [shards(): pl.pallas_call(kernel, out_shape=(jax.ShapeDtypeStruct(queries.shape, BF1...]
where the time goes in v4:
time: 68.4 us; the launch traced here: 68.1 us
  Pallas kernels  67.4 us (99%)
    pallas_call x1, Pallas kernels, shards(): pl.pallas_call(kernel, out_shape=(jax.ShapeDtypeStruct(queries.shape, BF1...  65.3 us
    pallas_call x1, Pallas kernels, shards(): pl.pallas_call(leave_kernel, out_shape=tuple((jax.ShapeDtypeStruct(v.shap...  2.1 us

profile of v4, /device:TPU:32, one launch (start us, length us, event | category | flops | bytes accessed | tf_op | source)
XLA Modules:
  0.0 68.1 jit_solution(12627963191434483874)
XLA Ops:
  0.6 65.3 %shard_map.92 = (bf16[2,64,1024]{2,1,0:T(8,128)(2,1)}, bf16[2,64,2048]{2,1,0:T(8,128)(2,1)}, bf16[2,64,1024]{2,1,0:T(8,128)(2,1)}, f32[16,512]{1,0:T(8,128)}, f32[16,512]{1,0:T(8,128)}) custom-call(bf16[2,64,2048]{2,1,0:T(8,128)(2,1)} %f_hbm.1, bf16[2,64,1024]{2,1,0:T(8,128)(2,1)} %q_hbm.1, bf16[2,64,1024]{2,1,0:T(8,128)(2,1)} %c_hbm.1, ...), custom_call_target="tpu_custom_call" | custom-call | tf_op jit(solution)/shard_map/pallas_call | solution.py:632
  66.0 2.1 %shard_map.93 = (bf16[2,64,1024]{2,1,0:T(8,128)(2,1)}, bf16[2,64,2048]{2,1,0:T(8,128)(2,1)}, bf16[2,64,1024]{2,1,0:T(8,128)(2,1)}, f32[16,512]{1,0:T(8,128)}, f32[16,512]{1,0:T(8,128)}) custom-call(bf16[2,64,1024]{2,1,0:T(8,128)(2,1)} %get-tuple-element.10.refs_0_, bf16[2,64,2048]{2,1,0:T(8,128)(2,1)} %get-tuple-element.11.refs_1_, ...), custom_call_target="tpu_custom_call" | custom-call | tf_op jit(solution)/shard_map/pallas_call | solution.py:648

commit v5 on v4

--- a/solution.py
+++ b/solution.py
@@ -124,7 +124,7 @@
 NT = NA + NB
 CW = 1024 - 128 * NT
 ORDER = (
-    "p01", "a01", "p00", "T0", "B0", "a00", "p10", "gfH", "p11", "F", "gf0", "T1", "gf", "c26",
+    "p01", "a01", "p00", "T0", "B0", "a00", "p10", "gfH", "p11", "F", "T1", "gf0", "gf", "c26",
     "B1", "S0", "S2", "S1", "S3", "c170", "T2", "H0", "H2", "H1", "H3", "a10", "a11", "home1",
     "home2", "B2", "T3", "M0", "M2", "M1", "M3", "Z", "C", "att", "gfout",
 )

time: 68.4 us -> 68.3 us (level)
  no operation moved by 1% of the time
where the time goes in v5:
time: 68.3 us; the launch traced here: 68.2 us
  Pallas kernels  67.6 us (99%)
    pallas_call x1, Pallas kernels, shards(): pl.pallas_call(kernel, out_shape=(jax.ShapeDtypeStruct(queries.shape, BF1...  65.5 us
    pallas_call x1, Pallas kernels, shards(): pl.pallas_call(leave_kernel, out_shape=tuple((jax.ShapeDtypeStruct(v.shap...  2.1 us

profile of v5, /device:TPU:32, one launch (start us, length us, event | category | flops | bytes accessed | tf_op | source)
XLA Modules:
  0.0 68.2 jit_solution(14170389430317728369)
XLA Ops:
  0.6 65.5 %shard_map.92 = (bf16[2,64,1024]{2,1,0:T(8,128)(2,1)}, bf16[2,64,2048]{2,1,0:T(8,128)(2,1)}, bf16[2,64,1024]{2,1,0:T(8,128)(2,1)}, f32[16,512]{1,0:T(8,128)}, f32[16,512]{1,0:T(8,128)}) custom-call(bf16[2,64,2048]{2,1,0:T(8,128)(2,1)} %f_hbm.1, bf16[2,64,1024]{2,1,0:T(8,128)(2,1)} %q_hbm.1, bf16[2,64,1024]{2,1,0:T(8,128)(2,1)} %c_hbm.1, ...), custom_call_target="tpu_custom_call" | custom-call | tf_op jit(solution)/shard_map/pallas_call | solution.py:632
  66.1 2.1 %shard_map.93 = (bf16[2,64,1024]{2,1,0:T(8,128)(2,1)}, bf16[2,64,2048]{2,1,0:T(8,128)(2,1)}, bf16[2,64,1024]{2,1,0:T(8,128)(2,1)}, f32[16,512]{1,0:T(8,128)}, f32[16,512]{1,0:T(8,128)}) custom-call(bf16[2,64,1024]{2,1,0:T(8,128)(2,1)} %get-tuple-element.10.refs_0_, bf16[2,64,2048]{2,1,0:T(8,128)(2,1)} %get-tuple-element.11.refs_1_, ...), custom_call_target="tpu_custom_call" | custom-call | tf_op jit(solution)/shard_map/pallas_call | solution.py:648

commit v6 on v5

--- a/solution.py
+++ b/solution.py
@@ -124,9 +124,9 @@
 NT = NA + NB
 CW = 1024 - 128 * NT
 ORDER = (
-    "p01", "a01", "p00", "T0", "B0", "a00", "p10", "gfH", "p11", "F", "T1", "gf0", "gf", "c26",
-    "B1", "S0", "S2", "S1", "S3", "c170", "T2", "H0", "H2", "H1", "H3", "a10", "a11", "home1",
-    "home2", "B2", "T3", "M0", "M2", "M1", "M3", "Z", "C", "att", "gfout",
+    "p01", "a01", "p00", "T0", "B0", "a00", "p10", "gfH", "p11", "F", "T1", "gf0", "c26", "B1",
+    "gf", "S0", "S2", "S1", "S3", "T2", "c170", "H0", "H2", "H1", "H3", "home1", "home2", "a10",
+    "a11", "B2", "T3", "M0", "M2", "M1", "M3", "Z", "C", "att", "gfout",
 )
 class Line4:
     def __init__(self, sends, mine, slices, devices, buf, sem, out):
@@ -250,11 +250,14 @@
         await_bytes(block, fsem.at[i])
         sends.start(block, block, got.at[1], base + c, 1 - s)
 
-    def project(lo):
+    def project(lo, pairs=(0, 1)):
         part = rows[lo : lo + 128, :]
-        k_scr[lo : lo + 128, :] = mm(part, kw[...], 1, 0).astype(BF16)
-        v_scr[lo : lo + 128, :] = mm(part, vw[...], 1, 0).astype(BF16)
-        rt[:, :, :, :, lo : lo + 128] = part.T.reshape(8, 4, 4, 16, 128)
+        for pair in pairs:
+            heads = slice(256 * pair, 256 * pair + 256)
+            k_scr[lo : lo + 128, heads] = mm(part, kw[:, heads], 1, 0).astype(BF16)
+            v_scr[lo : lo + 128, heads] = mm(part, vw[:, heads], 1, 0).astype(BF16)
+        if 0 in pairs:
+            rt[:, :, :, :, lo : lo + 128] = part.T.reshape(8, 4, 4, 16, 128)
 
     def other(lo):
         return rows_at(rows, lo + 64 * (1 - s), 64)
@@ -530,13 +533,14 @@
         else:
             halo_relay()
             await_bytes(other(0), got.at[2])
-            project(0)
+            project(0, (0,))
         attend(0, tile)
         if tile == 0:
             g[:, :512] = acc[:, :512].astype(BF16)
 
     def second_heads(tile):
         if tile == 0:
+            project(0, (1,))
             await_bytes(qc.at[1], qsem.at[1])
         attend(1, tile)
         if tile == 1:

time: 68.3 us -> 68.3 us (level)
  no operation moved by 1% of the time
where the time goes in v6:
time: 68.3 us; the launch traced here: 68 us
  Pallas kernels  67.4 us (99%)
    pallas_call x1, Pallas kernels, shards(): pl.pallas_call(kernel, out_shape=(jax.ShapeDtypeStruct(queries.shape, BF1...  65.3 us
    pallas_call x1, Pallas kernels, shards(): pl.pallas_call(leave_kernel, out_shape=tuple((jax.ShapeDtypeStruct(v.shap...  2.1 us

profile of v6, /device:TPU:32, one launch (start us, length us, event | category | flops | bytes accessed | tf_op | source)
XLA Modules:
  0.0 68.0 jit_solution(4322976698693175243)
XLA Ops:
  0.6 65.3 %shard_map.92 = (bf16[2,64,1024]{2,1,0:T(8,128)(2,1)}, bf16[2,64,2048]{2,1,0:T(8,128)(2,1)}, bf16[2,64,1024]{2,1,0:T(8,128)(2,1)}, f32[16,512]{1,0:T(8,128)}, f32[16,512]{1,0:T(8,128)}) custom-call(bf16[2,64,2048]{2,1,0:T(8,128)(2,1)} %f_hbm.1, bf16[2,64,1024]{2,1,0:T(8,128)(2,1)} %q_hbm.1, bf16[2,64,1024]{2,1,0:T(8,128)(2,1)} %c_hbm.1, ...), custom_call_target="tpu_custom_call" | custom-call | tf_op jit(solution)/shard_map/pallas_call | solution.py:636
  65.9 2.1 %shard_map.93 = (bf16[2,64,1024]{2,1,0:T(8,128)(2,1)}, bf16[2,64,2048]{2,1,0:T(8,128)(2,1)}, bf16[2,64,1024]{2,1,0:T(8,128)(2,1)}, f32[16,512]{1,0:T(8,128)}, f32[16,512]{1,0:T(8,128)}) custom-call(bf16[2,64,1024]{2,1,0:T(8,128)(2,1)} %get-tuple-element.10.refs_0_, bf16[2,64,2048]{2,1,0:T(8,128)(2,1)} %get-tuple-element.11.refs_1_, ...), custom_call_target="tpu_custom_call" | custom-call | tf_op jit(solution)/shard_map/pallas_call | solution.py:652

commit v7 on v5

--- a/solution.py
+++ b/solution.py
@@ -125,7 +125,7 @@
 CW = 1024 - 128 * NT
 ORDER = (
     "p01", "a01", "p00", "T0", "B0", "a00", "p10", "gfH", "p11", "F", "T1", "gf0", "gf", "c26",
-    "B1", "S0", "S2", "S1", "S3", "c170", "T2", "H0", "H2", "H1", "H3", "a10", "a11", "home1",
+    "B1", "S0", "S2", "S1", "S3", "T2", "c170", "H0", "H2", "H1", "H3", "a10", "a11", "home1",
     "home2", "B2", "T3", "M0", "M2", "M1", "M3", "Z", "C", "att", "gfout",
 )
 class Line4:

time: 68.3 us -> 68.3 us (level)
  no operation moved by 1% of the time
where the time goes in v7:
time: 68.3 us; the launch traced here: 68.2 us
  Pallas kernels  67.6 us (99%)
    pallas_call x1, Pallas kernels, shards(): pl.pallas_call(kernel, out_shape=(jax.ShapeDtypeStruct(queries.shape, BF1...  65.5 us
    pallas_call x1, Pallas kernels, shards(): pl.pallas_call(leave_kernel, out_shape=tuple((jax.ShapeDtypeStruct(v.shap...  2.1 us

profile of v7, /device:TPU:32, one launch (start us, length us, event | category | flops | bytes accessed | tf_op | source)
XLA Modules:
  0.0 68.2 jit_solution(10419985797647893550)
XLA Ops:
  0.6 65.5 %shard_map.92 = (bf16[2,64,1024]{2,1,0:T(8,128)(2,1)}, bf16[2,64,2048]{2,1,0:T(8,128)(2,1)}, bf16[2,64,1024]{2,1,0:T(8,128)(2,1)}, f32[16,512]{1,0:T(8,128)}, f32[16,512]{1,0:T(8,128)}) custom-call(bf16[2,64,2048]{2,1,0:T(8,128)(2,1)} %f_hbm.1, bf16[2,64,1024]{2,1,0:T(8,128)(2,1)} %q_hbm.1, bf16[2,64,1024]{2,1,0:T(8,128)(2,1)} %c_hbm.1, ...), custom_call_target="tpu_custom_call" | custom-call | tf_op jit(solution)/shard_map/pallas_call | solution.py:632
  66.1 2.1 %shard_map.93 = (bf16[2,64,1024]{2,1,0:T(8,128)(2,1)}, bf16[2,64,2048]{2,1,0:T(8,128)(2,1)}, bf16[2,64,1024]{2,1,0:T(8,128)(2,1)}, f32[16,512]{1,0:T(8,128)}, f32[16,512]{1,0:T(8,128)}) custom-call(bf16[2,64,1024]{2,1,0:T(8,128)(2,1)} %get-tuple-element.10.refs_0_, bf16[2,64,2048]{2,1,0:T(8,128)(2,1)} %get-tuple-element.11.refs_1_, ...), custom_call_target="tpu_custom_call" | custom-call | tf_op jit(solution)/shard_map/pallas_call | solution.py:648
